TPU v7x, 32 devices: a whole 2x2x4 slice. The times are simulated.
32 devices in a mesh: leaf: 8 (over z, y), top: 4 (over x, core).
Axes of the slice: x: 2, y: 2, z: 4, core: 2. Of those that a mesh axis runs over, the one named last changes fastest.
Arguments:
- coords: float32 [4, 8, 8, 4096], P('top', 'leaf'), may hold values from 0 to 1
- order: int32 [4, 8, 4096], P('top', 'leaf'), may hold values from 0 to 4095, each once within a row
- charges: bfloat16 [4, 8, 64, 4096], P('top', 'leaf'), may hold values from -6 to 6
- leaf_basis: bfloat16 [4, 8, 4, 128, 1024], P('top', 'leaf'), may hold values from -0.1875 to 0.1875
- leaf_factors: bfloat16 [4, 8, 4, 2, 2, 128, 128], P('top', 'leaf'), may hold values from -0.5 to 0.5
- transfer: bfloat16 [4, 8, 4, 128, 128], P('top', 'leaf'), may hold values from -0.5 to 0.5
- block_factors: bfloat16 [4, 8, 5, 2, 128, 128], P('top', 'leaf'), may hold values from -0.5 to 0.5
Outputs:
- potential: bfloat16 [4, 8, 64, 4096], P('top', 'leaf')
Inputs may be any that keep to these rules, and one draw needn't show every extreme that they name: Each block's row of order holds every number 0 to 4095 once.
All inputs are finite; a program needn't handle non-finite values.
Results may differ from a plain program's by a relative error of at most 0.0047.
Values sent between devices are 32-bit elements; how exact they have to be, the bound alone decides.
A program may use at most 64 MiB of HBM per device.

v0:
```python
import jax
import jax.numpy as jnp
from jax import lax
from jax.sharding import PartitionSpec as P

kernel_rate = 4.0
highest = lax.Precision.HIGHEST


def from_partner(x, axis, bit):
    return lax.ppermute(x, axis, [(i, i ^ 1 << bit) for i in range(lax.axis_size(axis))])


def kernel_block(points):
    sq_norms = jnp.sum(points * points, axis=0)
    inner_prod = lax.dot_general(
        points,
        points,
        (((0,), (0,)), ((), ())),
        precision=highest,
        preferred_element_type=jnp.float32,
    )
    return jnp.exp(
        -kernel_rate * (sq_norms[:, None] + sq_norms[None, :] - 2.0 * inner_prod)
    ).astype(jnp.bfloat16)


def near_leaf(pair_in):
    points, leaf_vals = pair_in
    kernel = kernel_block(points)
    return lax.dot_general(
        leaf_vals, kernel, (((1,), (1,)), ((), ())), preferred_element_type=jnp.float32
    )


def sibling_total(partial_value, height):
    nodes_len = partial_value.shape[0]
    subtree = 2**height
    grouped = partial_value.reshape(
        (nodes_len // (2 * subtree), 2, subtree) + partial_value.shape[1:]
    ).sum(axis=2)
    swapped = jnp.flip(grouped, axis=1)
    spread = jnp.broadcast_to(
        swapped[:, :, None], (nodes_len // (2 * subtree), 2, subtree) + partial_value.shape[1:]
    )
    return spread.reshape(partial_value.shape) * 0.5 ** (height / 2.0)


def local_terms(tree_vals, basis, factors, transfer):
    leaves = basis.shape[0]
    leaf_len = basis.shape[2]
    by_leaf = tree_vals.reshape(tree_vals.shape[0], leaves, leaf_len)
    skeleton = jnp.einsum("rjn,jkn->jrk", by_leaf, basis, preferred_element_type=jnp.float32)
    right_gen = factors[:, :, 0].astype(jnp.float32)
    left_gen = factors[:, :, 1].astype(jnp.float32)
    leaf_terms = jnp.einsum("jrk,jhkl->jhrl", skeleton, right_gen, precision=highest)
    coeffs = jnp.zeros(skeleton.shape, jnp.float32)
    for height in range(leaf_terms.shape[1]):
        summed = sibling_total(leaf_terms[:, height], height)
        coeffs = coeffs + jnp.einsum("jrk,jkl->jrl", summed, left_gen[:, height], precision=highest)
    block_sum = jnp.einsum("jrk,jkl->rl", skeleton, transfer.astype(jnp.float32), precision=highest)
    return (coeffs, block_sum)


def finish_block(perm_idx, values, points, basis, transfer, local_coeffs, block_coeffs):
    leaves = basis.shape[0]
    leaf_len = basis.shape[2]
    rhs_len = values.shape[0]
    tree_vals = values[:, perm_idx]
    tree_pts = points[:, perm_idx]
    leaf_vals = tree_vals.reshape(rhs_len, leaves, leaf_len).transpose(1, 0, 2)
    leaf_coords = tree_pts.reshape(points.shape[0], leaves, leaf_len).transpose(1, 0, 2)
    near = lax.map(near_leaf, (leaf_coords, leaf_vals))
    coeffs = local_coeffs + jnp.einsum(
        "rl,jkl->jrk", block_coeffs, transfer.astype(jnp.float32), precision=highest
    )
    coeffs = coeffs.astype(jnp.bfloat16)
    far = jnp.einsum("jrk,jkn->jrn", coeffs, basis, preferred_element_type=jnp.float32)
    field = (near + far).transpose(1, 0, 2).reshape(rhs_len, leaves * leaf_len).astype(jnp.bfloat16)
    return jnp.zeros((rhs_len, leaves * leaf_len), jnp.bfloat16).at[:, perm_idx].set(field)


def per_device(coords, order, charges, leaf_basis, leaf_factors, transfer, block_factors):
    perm_idx = order[0, 0]
    values = charges[0, 0]
    basis = leaf_basis[0, 0]
    trans_mat = transfer[0, 0]
    local_coeffs, block_sum = local_terms(values[:, perm_idx], basis, leaf_factors[0, 0], trans_mat)
    cross_gen = block_factors[0, 0].astype(jnp.float32)
    cross_terms = jnp.einsum("rk,hkl->hrl", block_sum, cross_gen[:, 0], precision=highest)
    leaf_bits = lax.axis_size("leaf").bit_length() - 1
    top_bits = lax.axis_size("top").bit_length() - 1
    pending = cross_terms
    sibling = []
    for level_bit in range(leaf_bits):
        received = from_partner(pending, "leaf", level_bit)
        sibling.append(received[0])
        pending = pending[1:] + received[1:]
    for level_bit in range(top_bits):
        received = from_partner(pending, "top", level_bit)
        sibling.append(received[0])
        pending = pending[1:] + received[1:]
    scales = jnp.array([0.5 ** (level_idx / 2.0) for level_idx in range(len(sibling))], jnp.float32)
    stacked = jnp.stack(sibling) * scales[:, None, None]
    block_coeffs = jnp.einsum("hrk,hkl->rl", stacked, cross_gen[:, 1], precision=highest)
    result = finish_block(
        perm_idx, values, coords[0, 0], basis, trans_mat, local_coeffs, block_coeffs
    )
    return result[None, None]


def solution(mesh):
    return jax.shard_map(
        per_device,
        mesh=mesh,
        in_specs=(
            P("top", "leaf", None, None),
            P("top", "leaf", None),
            P("top", "leaf", None, None),
            P("top", "leaf", None, None, None),
            P("top", "leaf", None, None, None, None, None),
            P("top", "leaf", None, None, None),
            P("top", "leaf", None, None, None, None),
        ),
        out_specs=P("top", "leaf", None, None),
        check_vma=False,
    )
```

profile of v0, /device:TPU:0, one launch (start us, length us, event | category | flops | bytes accessed | tf_op | source)
XLA Modules:
  0.0 97.4 jit_solution(10301910184794407477)
XLA Ops:
  0.0 0.8 compare_select_fusion
  0.8 1.5 %copy.17 = bf16[1,1,64,4096]{2,3,1,0:T(8,128)(2,1)S(1)} copy(bf16[1,1,64,4096]{3,2,1,0:T(8,128)(2,1)} %param.12) | data formatting | bytes 1048576 | tf_op args[2]
  2.4 1.0 %copy.33 = bf16[1,1,5,2,128,128]{5,4,2,3,1,0:T(8,128)(2,1)S(1)} copy(bf16[1,1,5,2,128,128]{5,4,3,2,1,0:T(8,128)(2,1)} %param.16) | data formatting | bytes 655360 | tf_op args[6]
  3.4 12.1 %gather_fusion = bf16[4096,64]{1,0:T(8,128)(2,1)S(1)} fusion(bf16[64,4096]{0,1:T(8,128)(2,1)S(1)} %bitcast.107, s32[4096]{0:T(1024)S(1)} %broadcast_clamp_fusion), kind=kCustom, calls=%fused_computation | custom fusion | bytes 1064960 | tf_op jit(solution)/shard_map/gather | solution.py:69
  16.6 0.9 convolution_bitcast_fusion.2
  17.5 3.0 %collective-permute-start = (f32[5,64,128]{2,1,0:T(8,128)}, f32[5,64,128]{2,1,0:T(8,128)}, u32[]{:S(2)}, u32[]{:S(2)}) collective-permute-start(f32[5,64,128]{2,1,0:T(8,128)} %convolution_bitcast_fusion.2), channel_id=1, source_target_pairs={{0,4},{4,0},{8,12},{12,8},{16,20},{20,16},{24,28},{28,24},{1,5},{5... | collective-permute-start | bytes 491528 | tf_op jit(solution)/shard_map/ppermute | solution.py:11
  20.8 0.7 slice_bitcast_fusion
  21.5 1.1 %copy.18 = bf16[64,4,1024]{2,0,1:T(8,128)(2,1)} copy(bf16[64,4,1024]{0,2,1:T(8,128)(2,1)S(1)} %bitcast.109) | data formatting | bytes 1048576 | tf_op jit(solution)/shard_map/reshape | solution.py:71
  23.3 0.7 rev.6
  24.0 1.5 %copy.19 = f32[1,1,8,4096]{2,3,1,0:T(8,128)S(1)} copy(f32[1,1,8,4096]{3,2,1,0:T(8,128)} %param.10) | data formatting | bytes 262144 | tf_op args[0]
  25.5 14.1 %gather_fusion.1 = f32[4096,8]{1,0:T(8,128)} fusion(f32[8,4096]{0,1:T(8,128)S(1)} %bitcast.110, s32[4096]{0:T(1024)S(1)} %broadcast_clamp_fusion), kind=kCustom, calls=%fused_computation.1 | custom fusion | bytes 278528 | tf_op jit(solution)/shard_map/gather | solution.py:70
  39.6 2.2 %copy.20 = f32[8,4,1024]{2,0,1:T(8,128)S(1)} copy(f32[8,4,1024]{0,2,1:T(8,128)} %bitcast.113) | data formatting | bytes 262144 | tf_op jit(solution)/shard_map/reshape | solution.py:72
  41.9 24.6 %while.10 = (s32[]{:T(128)}, f32[4,64,1024]{2,1,0:T(8,128)S(1)}, bf16[4,64,1024]{2,1,0:T(8,128)(2,1)}, f32[4,8,1024]{2,1,0:T(8,128)S(1)}, s32[]{:T(128)}) while((s32[]{:T(128)}, f32[4,64,1024]{2,1,0:T(8,128)S(1)}, bf16[4,64,1024]{2,1,0:T(8,128)(2,1)}, f32[4,8,1024]{2,1,0:T(8,128)S(1)}, s32[]{:T(128)}) %tuple.25), condition=%wide.region_2.3_spmd, body=%wide.region_0.2_spmd.sunk | while | flops 240139264 | bytes 4666437 | solution.py:73
  41.9 4.4 %exponential_convert_fusion.2 = bf16[1024,1024]{1,0:T(8,128)(2,1)S(1)} fusion(f32[1024]{0:T(1024)S(1)} %fusion.42, f32[4,8,1024]{2,1,0:T(8,128)S(1)} %get-tuple-element.78, s32[]{:T(128)} %get-tuple-element.70), kind=kOutput, calls=%fused_computation.3.clone.1 | convolution fusion | flops 105906176 | bytes 2138116 | tf_op jit(solution)/shard_map/while/body/eval_jaxpr/dot_general | solution.py:16
  46.3 1.7 %fusion.43 = f32[4,64,1024]{2,1,0:T(8,128)S(1)} fusion(f32[4,64,1024]{2,1,0:T(8,128)S(1)} %get-tuple-element.71, s32[]{:T(128)} %get-tuple-element.70, bf16[1024,1024]{1,0:T(8,128)(2,1)S(1)} %exponential_convert_fusion.2, bf16[4,64,1024]{2,1,0:T(8,128)(2,1)} %get-tuple-element.77), kind=kOutput, calls=%fused_computation.5.clone.1 | convolution fusion | flops 134217728 | bytes 2491392 | tf_op jit(solution)/shard_map/while/body/eval_jaxpr/dot_general | solution.py:31
  48.0 4.4 %exponential_convert_fusion.2 = bf16[1024,1024]{1,0:T(8,128)(2,1)S(1)} fusion(f32[1024]{0:T(1024)S(1)} %fusion.42, f32[4,8,1024]{2,1,0:T(8,128)S(1)} %get-tuple-element.78, s32[]{:T(128)} %get-tuple-element.70), kind=kOutput, calls=%fused_computation.3.clone.1 | convolution fusion | flops 105906176 | bytes 2138116 | tf_op jit(solution)/shard_map/while/body/eval_jaxpr/dot_general | solution.py:16
  52.5 1.7 %fusion.43 = f32[4,64,1024]{2,1,0:T(8,128)S(1)} fusion(f32[4,64,1024]{2,1,0:T(8,128)S(1)} %get-tuple-element.71, s32[]{:T(128)} %get-tuple-element.70, bf16[1024,1024]{1,0:T(8,128)(2,1)S(1)} %exponential_convert_fusion.2, bf16[4,64,1024]{2,1,0:T(8,128)(2,1)} %get-tuple-element.77), kind=kOutput, calls=%fused_computation.5.clone.1 | convolution fusion | flops 134217728 | bytes 2491392 | tf_op jit(solution)/shard_map/while/body/eval_jaxpr/dot_general | solution.py:31
  54.2 4.4 %exponential_convert_fusion.2 = bf16[1024,1024]{1,0:T(8,128)(2,1)S(1)} fusion(f32[1024]{0:T(1024)S(1)} %fusion.42, f32[4,8,1024]{2,1,0:T(8,128)S(1)} %get-tuple-element.78, s32[]{:T(128)} %get-tuple-element.70), kind=kOutput, calls=%fused_computation.3.clone.1 | convolution fusion | flops 105906176 | bytes 2138116 | tf_op jit(solution)/shard_map/while/body/eval_jaxpr/dot_general | solution.py:16
  58.6 1.7 %fusion.43 = f32[4,64,1024]{2,1,0:T(8,128)S(1)} fusion(f32[4,64,1024]{2,1,0:T(8,128)S(1)} %get-tuple-element.71, s32[]{:T(128)} %get-tuple-element.70, bf16[1024,1024]{1,0:T(8,128)(2,1)S(1)} %exponential_convert_fusion.2, bf16[4,64,1024]{2,1,0:T(8,128)(2,1)} %get-tuple-element.77), kind=kOutput, calls=%fused_computation.5.clone.1 | convolution fusion | flops 134217728 | bytes 2491392 | tf_op jit(solution)/shard_map/while/body/eval_jaxpr/dot_general | solution.py:31
  60.4 4.4 %exponential_convert_fusion.2 = bf16[1024,1024]{1,0:T(8,128)(2,1)S(1)} fusion(f32[1024]{0:T(1024)S(1)} %fusion.42, f32[4,8,1024]{2,1,0:T(8,128)S(1)} %get-tuple-element.78, s32[]{:T(128)} %get-tuple-element.70), kind=kOutput, calls=%fused_computation.3.clone.1 | convolution fusion | flops 105906176 | bytes 2138116 | tf_op jit(solution)/shard_map/while/body/eval_jaxpr/dot_general | solution.py:16
  64.8 1.7 %fusion.43 = f32[4,64,1024]{2,1,0:T(8,128)S(1)} fusion(f32[4,64,1024]{2,1,0:T(8,128)S(1)} %get-tuple-element.71, s32[]{:T(128)} %get-tuple-element.70, bf16[1024,1024]{1,0:T(8,128)(2,1)S(1)} %exponential_convert_fusion.2, bf16[4,64,1024]{2,1,0:T(8,128)(2,1)} %get-tuple-element.77), kind=kOutput, calls=%fused_computation.5.clone.1 | convolution fusion | flops 134217728 | bytes 2491392 | tf_op jit(solution)/shard_map/while/body/eval_jaxpr/dot_general | solution.py:31
  66.8 1.0 %slice_add_fusion = f32[4,64,128]{2,1,0:T(8,128)S(1)} fusion(f32[5,64,128]{2,1,0:T(8,128)} %collective-permute-done, f32[5,64,128]{2,1,0:T(8,128)} %convolution_bitcast_fusion.2), kind=kLoop, calls=%fused_computation.36 | loop fusion | flops 32768 | bytes 393216 | tf_op jit(solution)/shard_map/add | solution.py:98
  67.8 1.7 %collective-permute-start.1 = (f32[4,64,128]{2,1,0:T(8,128)S(1)}, f32[4,64,128]{2,1,0:T(8,128)S(1)}, u32[]{:S(2)}, u32[]{:S(2)}) collective-permute-start(f32[4,64,128]{2,1,0:T(8,128)S(1)} %slice_add_fusion), channel_id=1, source_target_pairs={{0,8},{4,12},{8,0},{12,4},{16,24},{20,28},{24,16},{28,20},{1,9},{5... | collective-permute-start | bytes 393224 | tf_op jit(solution)/shard_map/ppermute | solution.py:11
  69.4 0.8 slice_dynamic-update-slice_fusion.3
  70.2 2.6 %collective-permute-done.1 = f32[4,64,128]{2,1,0:T(8,128)S(1)} collective-permute-done((f32[4,64,128]{2,1,0:T(8,128)S(1)}, f32[4,64,128]{2,1,0:T(8,128)S(1)}, u32[]{:S(2)}, u32[]{:S(2)}) %collective-permute-start.1) | collective-permute-done | bytes 131104 | tf_op jit(solution)/shard_map/ppermute | solution.py:11
  72.8 2.6 %collective-permute-start.2 = (f32[3,64,128]{2,1,0:T(8,128)S(1)}, f32[3,64,128]{2,1,0:T(8,128)S(1)}, u32[]{:S(2)}, u32[]{:S(2)}) collective-permute-start(f32[3,64,128]{2,1,0:T(8,128)S(1)} %slice_add_fusion.1), channel_id=1, source_target_pairs={{0,16},{4,20},{8,24},{12,28},{16,0},{20,4},{24,8},{28,12},{1,17},{... | collective-permute-start | bytes 294920 | tf_op jit(solution)/shard_map/ppermute | solution.py:11
  75.5 2.9 %collective-permute-done.2 = f32[3,64,128]{2,1,0:T(8,128)S(1)} collective-permute-done((f32[3,64,128]{2,1,0:T(8,128)S(1)}, f32[3,64,128]{2,1,0:T(8,128)S(1)}, u32[]{:S(2)}, u32[]{:S(2)}) %collective-permute-start.2) | collective-permute-done | bytes 98336 | tf_op jit(solution)/shard_map/ppermute | solution.py:11
  78.5 1.2 %collective-permute-done.3 = f32[2,64,128]{2,1,0:T(8,128)S(1)} collective-permute-done((f32[2,64,128]{2,1,0:T(8,128)S(1)}, f32[2,64,128]{2,1,0:T(8,128)S(1)}, u32[]{:S(2)}, u32[]{:S(2)}) %collective-permute-start.3) | collective-permute-done | bytes 65568 | tf_op jit(solution)/shard_map/ppermute | solution.py:11
  79.8 1.6 %collective-permute-start.4 = (f32[1,64,128]{2,1,0:T(8,128)S(1)}, f32[1,64,128]{2,1,0:T(8,128)S(1)}, u32[]{:S(2)}, u32[]{:S(2)}) collective-permute-start(f32[1,64,128]{2,1,0:T(8,128)S(1)} %get-tuple-element.38), channel_id=1, source_target_pairs={{0,2},{1,3},{2,0},{3,1},{4,6},{5,7},{6,4},{7,5},{8,10},{9,11},{10,... | collective-permute-start | bytes 98312 | tf_op jit(solution)/shard_map/ppermute | solution.py:11
  81.6 2.2 %collective-permute-done.4 = f32[1,64,128]{2,1,0:T(8,128)S(1)} collective-permute-done((f32[1,64,128]{2,1,0:T(8,128)S(1)}, f32[1,64,128]{2,1,0:T(8,128)S(1)}, u32[]{:S(2)}, u32[]{:S(2)}) %collective-permute-start.4) | collective-permute-done | bytes 32800 | tf_op jit(solution)/shard_map/ppermute | solution.py:11
  85.2 11.1 %scatter_custom_fusion = bf16[64,4096]{0,1:T(8,128)(2,1)S(1)} fusion(s32[4096]{0:T(1024)S(1)} %bitcast.125, bf16[4096,64]{1,0:T(8,128)(2,1)S(1)} %copy.25, bf16[]{:T(256)} %constant.5.clone.1), kind=kCustom, calls=%fused_computation.27 | custom fusion | bytes 524290 | tf_op jit(solution)/shard_map/scatter | solution.py:80
  96.3 1.1 %copy.26 = bf16[1,1,64,4096]{3,2,1,0:T(8,128)(2,1)} copy(bf16[1,1,64,4096]{2,3,1,0:T(8,128)(2,1)S(1)} %bitcast.111) | data formatting | bytes 1048576 | tf_op jit(solution)/shard_map/broadcast_in_dim | solution.py:109
  (47 shorter events, 4.1 us)
Async XLA Ops:
  0.0 15.5 %copy-start = (bf16[1,1,4,128,1024]{4,3,2,1,0:T(8,128)(2,1)S(1)}, bf16[1,1,4,128,1024]{4,3,2,1,0:T(8,128)(2,1)}, u32[]{:S(2)}) copy-start(bf16[1,1,4,128,1024]{4,3,2,1,0:T(8,128)(2,1)} %param.13) | copy-start | bytes 3145732
  15.5 0.9 copy-start.5
  15.5 4.9 %copy-start.4 = (bf16[1,1,4,2,2,128,128]{6,5,4,3,2,1,0:T(8,128)(2,1)S(1)}, bf16[1,1,4,2,2,128,128]{6,5,4,3,2,1,0:T(8,128)(2,1)}, u32[]{:S(2)}) copy-start(bf16[1,1,4,2,2,128,128]{6,5,4,3,2,1,0:T(8,128)(2,1)} %param.14) | copy-start | bytes 1572868
  17.5 49.3 %collective-permute-start = (f32[5,64,128]{2,1,0:T(8,128)}, f32[5,64,128]{2,1,0:T(8,128)}, u32[]{:S(2)}, u32[]{:S(2)}) collective-permute-start(f32[5,64,128]{2,1,0:T(8,128)} %convolution_bitcast_fusion.2), channel_id=1, source_target_pairs={{0,4},{4,0},{8,12},{12,8},{16,20},{20,16},{24,28},{28,24},{1,5},{5... | collective-permute-start | bytes 491528 | tf_op jit(solution)/shard_map/ppermute | solution.py:11
  39.6 2.2 %copy-start.2 = (f32[4,64,1024]{2,1,0:T(8,128)S(1)}, f32[4,64,1024]{2,1,0:T(8,128)}, u32[]{:S(2)}) copy-start(f32[4,64,1024]{2,1,0:T(8,128)} %custom-call.5) | copy-start | bytes 3145732
  41.8 24.7 %copy-start.1 = (bf16[4,2,128,128]{3,2,1,0:T(8,128)(2,1)S(1)}, bf16[4,2,128,128]{3,2,1,0:T(8,128)(2,1)}, u32[]{:S(2)}) copy-start(bf16[4,2,128,128]{3,2,1,0:T(8,128)(2,1)} %slice_bitcast_fusion) | copy-start | bytes 786436
  41.8 24.7 %copy-start.3 = (f32[2,2,64,128]{3,2,1,0:T(8,128)S(1)}, f32[2,2,64,128]{3,2,1,0:T(8,128)}, u32[]{:S(2)}) copy-start(f32[2,2,64,128]{3,2,1,0:T(8,128)} %rev.6) | copy-start | bytes 393220
  41.8 24.9 %copy-start.7 = (f32[4,1,64,128]{3,2,1,0:T(8,128)S(1)}, f32[4,1,64,128]{3,2,1,0:T(8,128)}, u32[]{:S(2)}) copy-start(f32[4,1,64,128]{3,2,1,0:T(8,128)} %get-tuple-element.36) | copy-start | bytes 393220
  66.5 17.3 %copy-start.8 = (f32[5]{0:T(128)S(1)}, f32[5]{0:T(128)}, u32[]{:S(2)}) copy-start(f32[5]{0:T(128)} %constant.9.clone) | copy-start | bytes 64
  66.5 17.6 %copy-start.6 = (bf16[1,1,4,128,128]{4,3,2,1,0:T(8,128)(2,1)S(1)}, bf16[1,1,4,128,128]{4,3,2,1,0:T(8,128)(2,1)}, u32[]{:S(2)}) copy-start(bf16[1,1,4,128,128]{4,3,2,1,0:T(8,128)(2,1)} %param.15) | copy-start | bytes 393220
  67.8 5.0 %collective-permute-start.1 = (f32[4,64,128]{2,1,0:T(8,128)S(1)}, f32[4,64,128]{2,1,0:T(8,128)S(1)}, u32[]{:S(2)}, u32[]{:S(2)}) collective-permute-start(f32[4,64,128]{2,1,0:T(8,128)S(1)} %slice_add_fusion), channel_id=1, source_target_pairs={{0,8},{4,12},{8,0},{12,4},{16,24},{20,28},{24,16},{28,20},{1,9},{5... | collective-permute-start | bytes 393224 | tf_op jit(solution)/shard_map/ppermute | solution.py:11
  72.8 5.6 %collective-permute-start.2 = (f32[3,64,128]{2,1,0:T(8,128)S(1)}, f32[3,64,128]{2,1,0:T(8,128)S(1)}, u32[]{:S(2)}, u32[]{:S(2)}) collective-permute-start(f32[3,64,128]{2,1,0:T(8,128)S(1)} %slice_add_fusion.1), channel_id=1, source_target_pairs={{0,16},{4,20},{8,24},{12,28},{16,0},{20,4},{24,8},{28,12},{1,17},{... | collective-permute-start | bytes 294920 | tf_op jit(solution)/shard_map/ppermute | solution.py:11
  78.5 1.3 %collective-permute-start.3 = (f32[2,64,128]{2,1,0:T(8,128)S(1)}, f32[2,64,128]{2,1,0:T(8,128)S(1)}, u32[]{:S(2)}, u32[]{:S(2)}) collective-permute-start(f32[2,64,128]{2,1,0:T(8,128)S(1)} %slice_add_fusion.2), channel_id=1, source_target_pairs={{0,1},{1,0},{2,3},{3,2},{4,5},{5,4},{6,7},{7,6},{8,9},{9,8},{10,11... | collective-permute-start | bytes 196616 | tf_op jit(solution)/shard_map/ppermute | solution.py:11
  79.8 4.0 %collective-permute-start.4 = (f32[1,64,128]{2,1,0:T(8,128)S(1)}, f32[1,64,128]{2,1,0:T(8,128)S(1)}, u32[]{:S(2)}, u32[]{:S(2)}) collective-permute-start(f32[1,64,128]{2,1,0:T(8,128)S(1)} %get-tuple-element.38), channel_id=1, source_target_pairs={{0,2},{1,3},{2,0},{3,1},{4,6},{5,7},{6,4},{7,5},{8,10},{9,11},{10,... | collective-permute-start | bytes 98312 | tf_op jit(solution)/shard_map/ppermute | solution.py:11
where the time goes:
time: 97.8 us; the launch traced here: 97.4 us
  local copies, waits for them, and re-layouts  49.7 us (51%)
  matrix products  27.6 us (28%)
  waiting for transfers between devices  8.95 us (9%)
  starting transfers between devices  8.9 us (9%)
  other arithmetic  1.94 us (2%)
    dot_general x4, matrix products, kernel_block(): lax.dot_general(points, points, (((0,), (0,)), ((), ())), precision=highe...  17.7 us
    gather x1, local copies, waits for them, and re-layouts, finish_block(): tree_pts = points[:, perm_idx]  14.1 us
    gather x1, local copies, waits for them, and re-layouts, finish_block(): tree_vals = values[:, perm_idx]  12.1 us
    scatter x1, local copies, waits for them, and re-layouts, finish_block(): jnp.zeros((rhs_len, leaves * leaf_len), jnp.bfloat16).at[:, perm_idx]  11.1 us
    ppermute x5, waiting for transfers between devices, from_partner(): lax.ppermute(x, axis, [(i, i ^ 1 << bit) for i in range(lax.axis_size(axi...  8.95 us
    ppermute x5, starting transfers between devices, from_partner(): lax.ppermute(x, axis, [(i, i ^ 1 << bit) for i in range(lax.axis_size(axi...  8.9 us
    dot_general x4, matrix products, near_leaf(): lax.dot_general(leaf_vals, kernel, (((1,), (1,)), ((), ())), preferred_el...  6.68 us
    unnamed x25, local copies, waits for them, and re-layouts  5.22 us
  transfers between devices with their start and end apart: 5, of which 4 were waited for; matrix products, arithmetic and copies ran while one was open for 48% of the time, Pallas kernels for 0%

commit v1 on v0

v1 whole, which is shorter than its diff:
```python
import functools

import jax
import jax.numpy as jnp
from jax import lax
from jax.experimental import pallas as pl
from jax.experimental.pallas import tpu as pltpu
from jax.sharding import PartitionSpec as P

kernel_rate = 4.0
WIDTH = 128
UNROLL = 32
ROWS = 256
MESH = pl.DeviceIdType.MESH
VMEM = pl.BlockSpec(memory_space=pltpu.VMEM)
SMEM = pl.BlockSpec(memory_space=pltpu.SMEM)
f32, bf16 = jnp.float32, jnp.bfloat16


def split3(x):
    hi = x.astype(bf16).astype(f32)
    mid = (x - hi).astype(bf16).astype(f32)
    lo = (x - hi - mid).astype(bf16).astype(f32)
    return hi, mid, lo


def dot(a, b, dims=((1,), (0,))):
    return lax.dot_general(a, b, (dims, ((), ())), preferred_element_type=f32)


def dot_split(x, w):
    hi = x.astype(bf16)
    lo = (x - hi.astype(f32)).astype(bf16)
    return dot(hi, w) + dot(lo, w)


def up_kernel(order, coords, charges, basis, transfer, factors, rows_out, skel_out, terms_out, src, dst):
    rhs, points = charges.shape
    dim = coords.shape[0]
    leaves, rank, leaf_len = basis.shape
    step = 512
    scale = (2.0 * kernel_rate) ** 0.5
    for start in range(0, points, step):
        cols = pl.ds(start, step)
        pts = coords[:, cols] * scale
        hi, mid, lo = split3(pts)
        n_hi, n_mid, n_lo = split3(-0.5 * jnp.sum(pts * pts, axis=0, keepdims=True))
        left = WIDTH - rhs - 6 * dim
        row = lax.broadcasted_iota(jnp.int32, (left, step), 0)
        tail = jnp.where(row < 6, 1.0, 0.0)
        tail = jnp.where(row == 0, n_hi, jnp.where(row == 1, n_mid, jnp.where(row == 2, n_lo, tail)))
        whole = jnp.concatenate([charges[:, cols].astype(f32), hi, hi, mid, hi, lo, mid, tail], axis=0)
        src[cols, :] = whole.T

    @pl.loop(0, points // UNROLL)
    def _(block):
        base = pl.multiple_of(block * UNROLL, UNROLL)
        got = [src[pl.ds(order[base + u], 1), :] for u in range(UNROLL)]
        for u in range(UNROLL):
            dst[pl.ds(base + u, 1), :] = got[u]

    total = jnp.zeros((rhs, rank), f32)
    for j in range(leaves):
        span = pl.ds(j * leaf_len, leaf_len)
        mine = dst[span, :].astype(bf16)
        rows_out[span, :] = mine
        skel = dot(basis[j], mine).T[:rhs]
        skel_out[j] = skel
        total = total + dot_split(skel, transfer[j])
    for k in range(factors.shape[0]):
        terms_out[k] = dot_split(total, factors[k, 0])


def partner(levels_leaf, k):
    axis, bit = ("leaf", k) if k < levels_leaf else ("top", k - levels_leaf)
    me, stride = lax.axis_index(axis), 2**bit
    return {axis: me + stride - 2 * stride * lax.rem(lax.div(me, stride), 2)}


def field_kernel(
    levels_leaf, rows, skel, terms, basis, leaf_factors, transfer, factors, out, right, local, got, held, send, recv
):
    levels, rhs, rank = terms.shape
    leaves, _, leaf_len = basis.shape
    barrier = pltpu.get_barrier_semaphore()
    for k in range(levels):
        pl.semaphore_signal(barrier, inc=1, device_id=partner(levels_leaf, k), device_id_type=MESH)
    pl.semaphore_wait(barrier, levels)

    copies = {}

    def start(k, level):
        copies[k, level] = pltpu.make_async_remote_copy(
            src_ref=terms.at[level] if k == 0 else held.at[k, level],
            dst_ref=got.at[k, level],
            send_sem=send.at[k, level],
            recv_sem=recv.at[k, level],
            device_id=partner(levels_leaf, k),
            device_id_type=MESH,
        )
        copies[k, level].start()

    for level in reversed(range(levels)):
        start(0, level)

    coeffs = [jnp.zeros((rhs, rank), f32)]

    def receive(k, level):
        copies[k, level].wait_recv()
        if level == k:
            coeffs[0] = coeffs[0] + dot_split(got[k, k] * 0.5 ** (k / 2.0), factors[k, 1])
        else:
            held[k + 1, level] = (terms[level] if k == 0 else held[k, level]) + got[k, level]
            start(k + 1, level)

    def right_rows(j):
        lane = lax.broadcasted_iota(jnp.int32, (WIDTH, WIDTH), 1)
        lane_in = lax.broadcasted_iota(jnp.int32, (WIDTH, WIDTH), 0)
        dim = 8
        tail = rhs + 6 * dim
        source = lane
        for slot, shift in ((1, dim), (2, -2 * dim), (3, dim), (4, -4 * dim)):
            low = rhs + slot * dim
            source = jnp.where((lane >= low) & (lane < low + dim), lane + shift, source)
        source = jnp.where((lane >= tail) & (lane < tail + 3), lane + 3, source)
        source = jnp.where((lane >= tail + 3) & (lane < tail + 6), lane - 3, source)
        source = jnp.where((lane < rhs) | (lane >= tail + 6), -1, source)
        chosen = jnp.where(lane_in == source, 1.0, 0.0).astype(bf16)
        span = pl.ds(j * leaf_len, leaf_len)
        right[span, :] = dot(rows[span, :], chosen).astype(bf16)

    def near(j, start_row):
        span = pl.ds(j * leaf_len, leaf_len)
        mine = pl.ds(j * leaf_len + start_row, ROWS)
        power = dot(rows[mine, :], right[span, :], ((1,), (1,)))
        out[mine, :] = dot(jnp.exp(power).astype(bf16), rows[span, :])

    def local_terms(h):
        width = 2**h
        part = [dot_split(skel[j], leaf_factors[j, h, 0]) for j in range(leaves)]
        for j in range(leaves):
            other = (j // width ^ 1) * width
            summed = part[other]
            for i in range(1, width):
                summed = summed + part[other + i]
            mine = dot_split(summed * 0.5 ** (h / 2.0), leaf_factors[j, h, 1])
            local[j] = mine if h == 0 else local[j] + mine

    tasks = [functools.partial(right_rows, j) for j in range(leaves)]
    tasks += [functools.partial(local_terms, h) for h in range(leaf_factors.shape[1])]
    tasks += [functools.partial(near, j, s) for j in range(leaves) for s in range(0, leaf_len, ROWS)]
    events = [(k, level) for k in range(levels) for level in reversed(range(k, levels))]
    done = 0
    for i, task in enumerate(tasks):
        task()
        while done < len(events) * (i + 1) // len(tasks):
            receive(*events[done])
            done += 1
    for copy in copies.values():
        copy.wait_send()

    hi = coeffs[0].astype(bf16)
    lo = (coeffs[0] - hi.astype(f32)).astype(bf16)
    for j in range(leaves):
        span = pl.ds(j * leaf_len, leaf_len)
        mine = dot(transfer[j], hi, ((1,), (1,))) + dot(transfer[j], lo, ((1,), (1,)))
        mine = (mine + local[j].T).astype(bf16)
        out[span, :rhs] = out[span, :rhs] + dot(basis[j], mine, ((0,), (0,)))


def place_kernel(order, field, out, dst):
    rhs, points = out.shape

    @pl.loop(0, points // UNROLL)
    def _(block):
        base = pl.multiple_of(block * UNROLL, UNROLL)
        got = [field[pl.ds(base + u, 1), :] for u in range(UNROLL)]
        for u in range(UNROLL):
            dst[pl.ds(order[base + u], 1), :] = got[u]

    step = 512
    for start in range(0, points, step):
        out[:, pl.ds(start, step)] = dst[pl.ds(start, step), :].T[:rhs].astype(bf16)


def params(**more):
    return pltpu.CompilerParams(vmem_limit_bytes=28 * 2**20, **more)


def per_device(coords, order, charges, leaf_basis, leaf_factors, transfer, block_factors):
    coords, order, charges, basis = coords[0, 0], order[0, 0], charges[0, 0], leaf_basis[0, 0]
    leaf_factors, transfer, factors = leaf_factors[0, 0], transfer[0, 0], block_factors[0, 0]
    rhs, points = charges.shape
    leaves, rank, leaf_len = basis.shape
    levels = factors.shape[0]
    rows, skel, terms = pl.pallas_call(
        up_kernel,
        out_shape=(
            jax.ShapeDtypeStruct((points, WIDTH), bf16),
            jax.ShapeDtypeStruct((leaves, rhs, rank), f32),
            jax.ShapeDtypeStruct((levels, rhs, rank), f32),
        ),
        in_specs=[SMEM] + [VMEM] * 5,
        out_specs=(VMEM, VMEM, VMEM),
        scratch_shapes=[pltpu.VMEM((points, WIDTH), f32), pltpu.VMEM((points, WIDTH), f32)],
        compiler_params=params(),
        name="up",
    )(order, coords, charges, basis, transfer, factors)
    levels_leaf = lax.axis_size("leaf").bit_length() - 1
    field = pl.pallas_call(
        functools.partial(field_kernel, levels_leaf),
        out_shape=jax.ShapeDtypeStruct((points, WIDTH), f32),
        in_specs=[VMEM] * 7,
        out_specs=VMEM,
        scratch_shapes=[
            pltpu.VMEM((points, WIDTH), bf16),
            pltpu.VMEM((leaves, rhs, rank), f32),
            pltpu.VMEM((levels, levels, rhs, rank), f32),
            pltpu.VMEM((levels, levels, rhs, rank), f32),
            pltpu.SemaphoreType.DMA((levels, levels)),
            pltpu.SemaphoreType.DMA((levels, levels)),
        ],
        compiler_params=params(collective_id=0, has_side_effects=True),
        name="field",
    )(rows, skel, terms, basis, leaf_factors, transfer, factors)
    result = pl.pallas_call(
        place_kernel,
        out_shape=jax.ShapeDtypeStruct((rhs, points), bf16),
        in_specs=[SMEM, VMEM],
        out_specs=VMEM,
        scratch_shapes=[pltpu.VMEM((points, WIDTH), f32)],
        compiler_params=params(),
        name="place",
    )(order, field)
    return result[None, None]


def solution(mesh):
    return jax.shard_map(
        per_device,
        mesh=mesh,
        in_specs=(
            P("top", "leaf", None, None),
            P("top", "leaf", None),
            P("top", "leaf", None, None),
            P("top", "leaf", None, None, None),
            P("top", "leaf", None, None, None, None, None),
            P("top", "leaf", None, None, None),
            P("top", "leaf", None, None, None, None),
        ),
        out_specs=P("top", "leaf", None, None),
        check_vma=False,
    )
```

time: 97.8 us -> 39.8 us (0.41)
  local copies, waits for them, and re-layouts: 49.7 us -> 5.78 us
  Pallas kernels: 0 us -> 33.7 us
  matrix products: 27.6 us -> 0 us
  waiting for transfers between devices: 8.95 us -> 0 us
  starting transfers between devices: 8.9 us -> 0 us
  other arithmetic: 1.94 us -> 0 us
    pallas_call x0 -> x3, Pallas kernels: none -> 33.7 us  [the longest x1 21.6 us: per_device(): pl.pallas_call(functools.partial(field_kernel, levels_leaf), out_shape=ja...]
    dot_general x17 -> x0, matrix products: 27.6 us -> none  [the longest x4 17.7 us: kernel_block(): lax.dot_general(points, points, (((0,), (0,)), ((), ())), precision=highe...]
    gather x2 -> x0, local copies, waits for them, and re-layouts: 26.2 us -> none  [the longest x1 14.1 us: finish_block(): tree_pts = points[:, perm_idx]]
    scatter x1 -> x0, local copies, waits for them, and re-layouts: 11.1 us -> none  [finish_block(): jnp.zeros((rhs_len, leaves * leaf_len), jnp.bfloat16).at[:, perm_idx]]
    ppermute x5 -> x0, waiting for transfers between devices: 8.95 us -> none  [from_partner(): lax.ppermute(x, axis, [(i, i ^ 1 << bit) for i in range(lax.axis_size(axi...]
    ppermute x5 -> x0, starting transfers between devices: 8.9 us -> none  [from_partner(): lax.ppermute(x, axis, [(i, i ^ 1 << bit) for i in range(lax.axis_size(axi...]
    reshape x2 -> x0, local copies, waits for them, and re-layouts: 3.37 us -> none  [the longest x1 2.24 us: finish_block(): tree_pts.reshape(points.shape[0], leaves, leaf_len).transpose(1, 0, 2)]
    broadcast_in_dim x2 -> x0, local copies, waits for them, and re-layouts: 1.14 us -> none  [the longest x1 1.13 us: per_device(): return result[None, None]]
  transfers between devices with their start and end apart: 5 -> 0, of which waited for: 4 -> 0; matrix products, arithmetic and copies ran while one was open for 48% -> 0% of each run, Pallas kernels for 0% -> 0%
where the time goes in v1:
time: 39.8 us; the launch traced here: 39.5 us
  Pallas kernels  33.7 us (85%)
  local copies, waits for them, and re-layouts  5.78 us (15%)
    pallas_call x1, Pallas kernels, per_device(): pl.pallas_call(functools.partial(field_kernel, levels_leaf), out_shape=ja...  21.6 us
    pallas_call x1, Pallas kernels, per_device(): pl.pallas_call(up_kernel, out_shape=(jax.ShapeDtypeStruct((points, WIDTH)...  6.32 us
    unnamed x18, local copies, waits for them, and re-layouts  5.78 us
    pallas_call x1, Pallas kernels, per_device(): pl.pallas_call(place_kernel, out_shape=jax.ShapeDtypeStruct((rhs, points)...  5.76 us

profile of v1, /device:TPU:0, one launch (start us, length us, event | category | flops | bytes accessed | tf_op | source)
XLA Modules:
  0.0 39.5 jit_solution(5693389840735829811)
XLA Ops:
  0.0 0.0 copy-start
  0.0 1.2 %copy-done = bf16[1,1,4,128,1024]{4,3,2,1,0:T(8,128)(2,1)S(1)} copy-done((bf16[1,1,4,128,1024]{4,3,2,1,0:T(8,128)(2,1)S(1)}, bf16[1,1,4,128,1024]{4,3,2,1,0:T(8,128)(2,1)}, u32[]{:S(2)}) %copy-start) | copy-done | bytes 1048600
  1.2 0.0 copy-start.2
  1.2 1.0 %copy-done.2 = bf16[1,1,5,2,128,128]{5,4,3,2,1,0:T(8,128)(2,1)S(1)} copy-done((bf16[1,1,5,2,128,128]{5,4,3,2,1,0:T(8,128)(2,1)S(1)}, bf16[1,1,5,2,128,128]{5,4,3,2,1,0:T(8,128)(2,1)}, u32[]{:S(2)}) %copy-start.2) | copy-done | bytes 327704
  2.2 0.0 copy-start.4
  2.2 0.9 %copy-done.4 = bf16[1,1,4,128,128]{4,3,2,1,0:T(8,128)(2,1)S(1)} copy-done((bf16[1,1,4,128,128]{4,3,2,1,0:T(8,128)(2,1)S(1)}, bf16[1,1,4,128,128]{4,3,2,1,0:T(8,128)(2,1)}, u32[]{:S(2)}) %copy-start.4) | copy-done | bytes 131096
  3.1 0.0 copy-start.5
  3.1 1.0 %copy-done.5 = bf16[1,1,64,4096]{3,2,1,0:T(8,128)(2,1)S(1)} copy-done((bf16[1,1,64,4096]{3,2,1,0:T(8,128)(2,1)S(1)}, bf16[1,1,64,4096]{3,2,1,0:T(8,128)(2,1)}, u32[]{:S(2)}) %copy-start.5) | copy-done | bytes 524312
  4.1 0.0 copy-start.7
  4.1 0.9 %copy-done.7 = f32[1,1,8,4096]{3,2,1,0:T(8,128)S(1)} copy-done((f32[1,1,8,4096]{3,2,1,0:T(8,128)S(1)}, f32[1,1,8,4096]{3,2,1,0:T(8,128)}, u32[]{:S(2)}) %copy-start.7) | copy-done | bytes 131096
  5.1 0.0 copy-start.8
  5.1 0.7 %copy-done.8 = s32[1,1,4096]{2,1,0:T(1,128)S(1)} copy-done((s32[1,1,4096]{2,1,0:T(1,128)S(1)}, s32[1,1,4096]{2,1,0:T(1,128)}, u32[]{:S(2)}) %copy-start.8) | copy-done | bytes 16408
  5.8 0.0 copy-start.1
  5.8 0.0 copy-start.3
  5.8 0.0 copy-start.6
  5.8 6.3 %up.1 = (bf16[4096,128]{1,0:T(8,128)(2,1)S(1)}, f32[4,64,128]{2,1,0:T(8,128)S(1)}, f32[5,64,128]{2,1,0:T(8,128)S(1)}) custom-call(s32[4096]{0:T(1024)S(1)} %bitcast.17, f32[8,4096]{1,0:T(8,128)S(1)} %bitcast.16, bf16[64,4096]{1,0:T(8,128)(2,1)S(1)} %bitcast.14, bf16[4,128,1024]{2,1,0:T(8,128)(2,1)S(1)} %bitcast.8, bf16[4,128,128]{2,1,0:T(8,128)(2,1)S(1)} %bitcast.12, ...), custom_call_target="tpu_custom_call" | custom-call | tf_op jit(solution)/shard_map/up/pallas_call | solution.py:196
  12.1 0.0 copy-done.1
  12.1 0.0 copy-done.3
  12.1 0.0 copy-done.6
  12.1 21.6 %field.1 = f32[4096,128]{1,0:T(8,128)S(1)} custom-call(bf16[4096,128]{1,0:T(8,128)(2,1)S(1)} %get-tuple-element.8.rows, f32[4,64,128]{2,1,0:T(8,128)S(1)} %get-tuple-element.9.skel, f32[5,64,128]{2,1,0:T(8,128)S(1)} %get-tuple-element.10.terms, bf16[4,128,1024]{2,1,0:T(8,128)(2,1)S(1)} %bitcast.9, bf16[4,2,2,128,128]{4,3,2,1,0:T(8,128)(2,1)S(1)} %bitcast.15, ...), custom_call_target="tpu_custom_call" | custom-call | tf_op jit(solution)/shard_map/field/pallas_call | solution.py:210
  33.7 5.8 %place.1 = bf16[64,4096]{1,0:T(8,128)(2,1)} custom-call(s32[4096]{0:T(1024)S(1)} %bitcast.18, f32[4096,128]{1,0:T(8,128)S(1)} %field.1), custom_call_target="tpu_custom_call" | custom-call | tf_op jit(solution)/shard_map/place/pallas_call | solution.py:226
Async XLA Ops:
  0.0 1.2 %copy-start = (bf16[1,1,4,128,1024]{4,3,2,1,0:T(8,128)(2,1)S(1)}, bf16[1,1,4,128,1024]{4,3,2,1,0:T(8,128)(2,1)}, u32[]{:S(2)}) copy-start(bf16[1,1,4,128,1024]{4,3,2,1,0:T(8,128)(2,1)} %param.10) | copy-start | bytes 3145732
  1.2 1.0 %copy-start.2 = (bf16[1,1,5,2,128,128]{5,4,3,2,1,0:T(8,128)(2,1)S(1)}, bf16[1,1,5,2,128,128]{5,4,3,2,1,0:T(8,128)(2,1)}, u32[]{:S(2)}) copy-start(bf16[1,1,5,2,128,128]{5,4,3,2,1,0:T(8,128)(2,1)} %param.13) | copy-start | bytes 983044
  2.2 0.9 %copy-start.4 = (bf16[1,1,4,128,128]{4,3,2,1,0:T(8,128)(2,1)S(1)}, bf16[1,1,4,128,128]{4,3,2,1,0:T(8,128)(2,1)}, u32[]{:S(2)}) copy-start(bf16[1,1,4,128,128]{4,3,2,1,0:T(8,128)(2,1)} %param.12) | copy-start | bytes 393220
  3.1 1.0 %copy-start.5 = (bf16[1,1,64,4096]{3,2,1,0:T(8,128)(2,1)S(1)}, bf16[1,1,64,4096]{3,2,1,0:T(8,128)(2,1)}, u32[]{:S(2)}) copy-start(bf16[1,1,64,4096]{3,2,1,0:T(8,128)(2,1)} %param.9) | copy-start | bytes 1572868
  4.1 0.9 %copy-start.7 = (f32[1,1,8,4096]{3,2,1,0:T(8,128)S(1)}, f32[1,1,8,4096]{3,2,1,0:T(8,128)}, u32[]{:S(2)}) copy-start(f32[1,1,8,4096]{3,2,1,0:T(8,128)} %param.7) | copy-start | bytes 393220
  5.1 0.7 %copy-start.8 = (s32[1,1,4096]{2,1,0:T(1,128)S(1)}, s32[1,1,4096]{2,1,0:T(1,128)}, u32[]{:S(2)}) copy-start(s32[1,1,4096]{2,1,0:T(1,128)} %param.8) | copy-start | bytes 49156
  5.8 6.3 %copy-start.1 = (bf16[1,1,4,128,1024]{4,3,2,1,0:T(8,128)(2,1)S(1)}, bf16[1,1,4,128,1024]{4,3,2,1,0:T(8,128)(2,1)}, u32[]{:S(2)}) copy-start(bf16[1,1,4,128,1024]{4,3,2,1,0:T(8,128)(2,1)} %param.10) | copy-start | bytes 3145732
  5.8 6.3 %copy-start.3 = (bf16[1,1,5,2,128,128]{5,4,3,2,1,0:T(8,128)(2,1)S(1)}, bf16[1,1,5,2,128,128]{5,4,3,2,1,0:T(8,128)(2,1)}, u32[]{:S(2)}) copy-start(bf16[1,1,5,2,128,128]{5,4,3,2,1,0:T(8,128)(2,1)} %param.13) | copy-start | bytes 983044
  5.8 6.3 %copy-start.6 = (bf16[1,1,4,2,2,128,128]{6,5,4,3,2,1,0:T(8,128)(2,1)S(1)}, bf16[1,1,4,2,2,128,128]{6,5,4,3,2,1,0:T(8,128)(2,1)}, u32[]{:S(2)}) copy-start(bf16[1,1,4,2,2,128,128]{6,5,4,3,2,1,0:T(8,128)(2,1)} %param.11) | copy-start | bytes 1572868

commit v2 on v1

--- a/solution.py
+++ b/solution.py
@@ -34,7 +34,15 @@
     return dot(hi, w) + dot(lo, w)
 
 
-def up_kernel(order, coords, charges, basis, transfer, factors, rows_out, skel_out, terms_out, src, dst):
+def up_kernel(*refs):
+    given, (rows_out, skel_out, terms_out), (src, dst) = refs[:6], refs[6:9], refs[9:11]
+    held, sems = refs[11:17], refs[17]
+    order, coords, charges, basis, transfer, factors = held
+    copies = [pltpu.make_async_copy(a, b, sems.at[i]) for i, (a, b) in enumerate(zip(given, held))]
+    for i in (1, 2, 0, 3, 4, 5):
+        copies[i].start()
+    copies[1].wait()
+    copies[2].wait()
     rhs, points = charges.shape
     dim = coords.shape[0]
     leaves, rank, leaf_len = basis.shape
@@ -52,6 +60,8 @@
         whole = jnp.concatenate([charges[:, cols].astype(f32), hi, hi, mid, hi, lo, mid, tail], axis=0)
         src[cols, :] = whole.T
 
+    copies[0].wait()
+
     @pl.loop(0, points // UNROLL)
     def _(block):
         base = pl.multiple_of(block * UNROLL, UNROLL)
@@ -59,6 +69,8 @@
         for u in range(UNROLL):
             dst[pl.ds(base + u, 1), :] = got[u]
 
+    for i in (3, 4, 5):
+        copies[i].wait()
     total = jnp.zeros((rhs, rank), f32)
     for j in range(leaves):
         span = pl.ds(j * leaf_len, leaf_len)
@@ -149,11 +161,13 @@
     tasks = [functools.partial(right_rows, j) for j in range(leaves)]
     tasks += [functools.partial(local_terms, h) for h in range(leaf_factors.shape[1])]
     tasks += [functools.partial(near, j, s) for j in range(leaves) for s in range(0, leaf_len, ROWS)]
-    events = [(k, level) for k in range(levels) for level in reversed(range(k, levels))]
+    events = [(k, level) for k in range(levels) for level in range(k, levels)]
+    events.sort(key=lambda event: (2 * event[0] + levels - 1 - event[1], event[0]))
+    first = leaves + leaf_factors.shape[1]
     done = 0
     for i, task in enumerate(tasks):
         task()
-        while done < len(events) * (i + 1) // len(tasks):
+        while done < len(events) * (i + 1 - first) // (len(tasks) - first):
             receive(*events[done])
             done += 1
     for copy in copies.values():
@@ -200,9 +214,15 @@
             jax.ShapeDtypeStruct((leaves, rhs, rank), f32),
             jax.ShapeDtypeStruct((levels, rhs, rank), f32),
         ),
-        in_specs=[SMEM] + [VMEM] * 5,
+        in_specs=[pl.BlockSpec(memory_space=pltpu.HBM)] * 6,
         out_specs=(VMEM, VMEM, VMEM),
-        scratch_shapes=[pltpu.VMEM((points, WIDTH), f32), pltpu.VMEM((points, WIDTH), f32)],
+        scratch_shapes=[
+            pltpu.VMEM((points, WIDTH), f32),
+            pltpu.VMEM((points, WIDTH), f32),
+            pltpu.SMEM(order.shape, order.dtype),
+            *[pltpu.VMEM(a.shape, a.dtype) for a in (coords, charges, basis, transfer, factors)],
+            pltpu.SemaphoreType.DMA((6,)),
+        ],
         compiler_params=params(),
         name="up",
     )(order, coords, charges, basis, transfer, factors)

time: 39.8 us -> 39.2 us (0.985)
  Pallas kernels: 33.7 us -> 33.1 us
    pallas_call x1, Pallas kernels: 21.6 us -> 21.1 us  [per_device(): pl.pallas_call(functools.partial(field_kernel, levels_leaf), out_shape=ja...]
where the time goes in v2:
time: 39.2 us; the launch traced here: 38.9 us
  Pallas kernels  33.1 us (84%)
  local copies, waits for them, and re-layouts  5.77 us (15%)
    pallas_call x1, Pallas kernels, per_device(): pl.pallas_call(functools.partial(field_kernel, levels_leaf), out_shape=ja...  21.1 us
    pallas_call x1, Pallas kernels, per_device(): pl.pallas_call(up_kernel, out_shape=(jax.ShapeDtypeStruct((points, WIDTH)...  6.23 us
    unnamed x18, local copies, waits for them, and re-layouts  5.77 us
    pallas_call x1, Pallas kernels, per_device(): pl.pallas_call(place_kernel, out_shape=jax.ShapeDtypeStruct((rhs, points)...  5.76 us

profile of v2, /device:TPU:0, one launch (start us, length us, event | category | flops | bytes accessed | tf_op | source)
XLA Modules:
  0.0 38.9 jit_solution(13758435480330975418)
XLA Ops:
  0.0 0.0 copy-start
  0.0 1.2 %copy-done = bf16[1,1,4,128,1024]{4,3,2,1,0:T(8,128)(2,1)S(1)} copy-done((bf16[1,1,4,128,1024]{4,3,2,1,0:T(8,128)(2,1)S(1)}, bf16[1,1,4,128,1024]{4,3,2,1,0:T(8,128)(2,1)}, u32[]{:S(2)}) %copy-start) | copy-done | bytes 1048600
  1.2 0.0 copy-start.2
  1.2 1.0 %copy-done.2 = bf16[1,1,5,2,128,128]{5,4,3,2,1,0:T(8,128)(2,1)S(1)} copy-done((bf16[1,1,5,2,128,128]{5,4,3,2,1,0:T(8,128)(2,1)S(1)}, bf16[1,1,5,2,128,128]{5,4,3,2,1,0:T(8,128)(2,1)}, u32[]{:S(2)}) %copy-start.2) | copy-done | bytes 327704
  2.2 0.0 copy-start.4
  2.2 0.9 %copy-done.4 = bf16[1,1,4,128,128]{4,3,2,1,0:T(8,128)(2,1)S(1)} copy-done((bf16[1,1,4,128,128]{4,3,2,1,0:T(8,128)(2,1)S(1)}, bf16[1,1,4,128,128]{4,3,2,1,0:T(8,128)(2,1)}, u32[]{:S(2)}) %copy-start.4) | copy-done | bytes 131096
  3.1 0.0 copy-start.5
  3.1 1.0 %copy-done.5 = bf16[1,1,64,4096]{3,2,1,0:T(8,128)(2,1)S(1)} copy-done((bf16[1,1,64,4096]{3,2,1,0:T(8,128)(2,1)S(1)}, bf16[1,1,64,4096]{3,2,1,0:T(8,128)(2,1)}, u32[]{:S(2)}) %copy-start.5) | copy-done | bytes 524312
  4.1 0.0 copy-start.7
  4.1 0.9 %copy-done.7 = f32[1,1,8,4096]{3,2,1,0:T(8,128)S(1)} copy-done((f32[1,1,8,4096]{3,2,1,0:T(8,128)S(1)}, f32[1,1,8,4096]{3,2,1,0:T(8,128)}, u32[]{:S(2)}) %copy-start.7) | copy-done | bytes 131096
  5.1 0.0 copy-start.8
  5.1 0.7 %copy-done.8 = s32[1,1,4096]{2,1,0:T(1,128)S(1)} copy-done((s32[1,1,4096]{2,1,0:T(1,128)S(1)}, s32[1,1,4096]{2,1,0:T(1,128)}, u32[]{:S(2)}) %copy-start.8) | copy-done | bytes 16408
  5.8 0.0 copy-start.1
  5.8 0.0 copy-start.3
  5.8 0.0 copy-start.6
  5.8 6.2 %up.1 = (bf16[4096,128]{1,0:T(8,128)(2,1)S(1)}, f32[4,64,128]{2,1,0:T(8,128)S(1)}, f32[5,64,128]{2,1,0:T(8,128)S(1)}) custom-call(s32[4096]{0:T(1024)S(1)} %bitcast.17, f32[8,4096]{1,0:T(8,128)S(1)} %bitcast.16, bf16[64,4096]{1,0:T(8,128)(2,1)S(1)} %bitcast.14, bf16[4,128,1024]{2,1,0:T(8,128)(2,1)S(1)} %bitcast.8, bf16[4,128,128]{2,1,0:T(8,128)(2,1)S(1)} %bitcast.12, ...), custom_call_target="tpu_custom_call" | custom-call | tf_op jit(solution)/shard_map/up/pallas_call | solution.py:210
  12.0 0.0 copy-done.1
  12.0 0.0 copy-done.3
  12.0 0.0 copy-done.6
  12.0 21.1 %field.1 = f32[4096,128]{1,0:T(8,128)S(1)} custom-call(bf16[4096,128]{1,0:T(8,128)(2,1)S(1)} %get-tuple-element.8.rows, f32[4,64,128]{2,1,0:T(8,128)S(1)} %get-tuple-element.9.skel, f32[5,64,128]{2,1,0:T(8,128)S(1)} %get-tuple-element.10.terms, bf16[4,128,1024]{2,1,0:T(8,128)(2,1)S(1)} %bitcast.9, bf16[4,2,2,128,128]{4,3,2,1,0:T(8,128)(2,1)S(1)} %bitcast.15, ...), custom_call_target="tpu_custom_call" | custom-call | tf_op jit(solution)/shard_map/field/pallas_call | solution.py:230
  33.1 5.8 %place.1 = bf16[64,4096]{1,0:T(8,128)(2,1)} custom-call(s32[4096]{0:T(1024)S(1)} %bitcast.18, f32[4096,128]{1,0:T(8,128)S(1)} %field.1), custom_call_target="tpu_custom_call" | custom-call | tf_op jit(solution)/shard_map/place/pallas_call | solution.py:246
Async XLA Ops:
  0.0 1.2 %copy-start = (bf16[1,1,4,128,1024]{4,3,2,1,0:T(8,128)(2,1)S(1)}, bf16[1,1,4,128,1024]{4,3,2,1,0:T(8,128)(2,1)}, u32[]{:S(2)}) copy-start(bf16[1,1,4,128,1024]{4,3,2,1,0:T(8,128)(2,1)} %param.10) | copy-start | bytes 3145732
  1.2 1.0 %copy-start.2 = (bf16[1,1,5,2,128,128]{5,4,3,2,1,0:T(8,128)(2,1)S(1)}, bf16[1,1,5,2,128,128]{5,4,3,2,1,0:T(8,128)(2,1)}, u32[]{:S(2)}) copy-start(bf16[1,1,5,2,128,128]{5,4,3,2,1,0:T(8,128)(2,1)} %param.13) | copy-start | bytes 983044
  2.2 0.9 %copy-start.4 = (bf16[1,1,4,128,128]{4,3,2,1,0:T(8,128)(2,1)S(1)}, bf16[1,1,4,128,128]{4,3,2,1,0:T(8,128)(2,1)}, u32[]{:S(2)}) copy-start(bf16[1,1,4,128,128]{4,3,2,1,0:T(8,128)(2,1)} %param.12) | copy-start | bytes 393220
  3.1 1.0 %copy-start.5 = (bf16[1,1,64,4096]{3,2,1,0:T(8,128)(2,1)S(1)}, bf16[1,1,64,4096]{3,2,1,0:T(8,128)(2,1)}, u32[]{:S(2)}) copy-start(bf16[1,1,64,4096]{3,2,1,0:T(8,128)(2,1)} %param.9) | copy-start | bytes 1572868
  4.1 0.9 %copy-start.7 = (f32[1,1,8,4096]{3,2,1,0:T(8,128)S(1)}, f32[1,1,8,4096]{3,2,1,0:T(8,128)}, u32[]{:S(2)}) copy-start(f32[1,1,8,4096]{3,2,1,0:T(8,128)} %param.7) | copy-start | bytes 393220
  5.1 0.7 %copy-start.8 = (s32[1,1,4096]{2,1,0:T(1,128)S(1)}, s32[1,1,4096]{2,1,0:T(1,128)}, u32[]{:S(2)}) copy-start(s32[1,1,4096]{2,1,0:T(1,128)} %param.8) | copy-start | bytes 49156
  5.8 6.2 %copy-start.1 = (bf16[1,1,4,128,1024]{4,3,2,1,0:T(8,128)(2,1)S(1)}, bf16[1,1,4,128,1024]{4,3,2,1,0:T(8,128)(2,1)}, u32[]{:S(2)}) copy-start(bf16[1,1,4,128,1024]{4,3,2,1,0:T(8,128)(2,1)} %param.10) | copy-start | bytes 3145732
  5.8 6.3 %copy-start.3 = (bf16[1,1,5,2,128,128]{5,4,3,2,1,0:T(8,128)(2,1)S(1)}, bf16[1,1,5,2,128,128]{5,4,3,2,1,0:T(8,128)(2,1)}, u32[]{:S(2)}) copy-start(bf16[1,1,5,2,128,128]{5,4,3,2,1,0:T(8,128)(2,1)} %param.13) | copy-start | bytes 983044
  5.8 6.3 %copy-start.6 = (bf16[1,1,4,2,2,128,128]{6,5,4,3,2,1,0:T(8,128)(2,1)S(1)}, bf16[1,1,4,2,2,128,128]{6,5,4,3,2,1,0:T(8,128)(2,1)}, u32[]{:S(2)}) copy-start(bf16[1,1,4,2,2,128,128]{6,5,4,3,2,1,0:T(8,128)(2,1)} %param.11) | copy-start | bytes 1572868

commit v3 on v1

--- a/solution.py
+++ b/solution.py
@@ -34,10 +34,9 @@
     return dot(hi, w) + dot(lo, w)
 
 
-def up_kernel(order, coords, charges, basis, transfer, factors, rows_out, skel_out, terms_out, src, dst):
+def gather_kernel(order, coords, charges, rows_out, src, dst):
     rhs, points = charges.shape
     dim = coords.shape[0]
-    leaves, rank, leaf_len = basis.shape
     step = 512
     scale = (2.0 * kernel_rate) ** 0.5
     for start in range(0, points, step):
@@ -59,16 +58,7 @@
         for u in range(UNROLL):
             dst[pl.ds(base + u, 1), :] = got[u]
 
-    total = jnp.zeros((rhs, rank), f32)
-    for j in range(leaves):
-        span = pl.ds(j * leaf_len, leaf_len)
-        mine = dst[span, :].astype(bf16)
-        rows_out[span, :] = mine
-        skel = dot(basis[j], mine).T[:rhs]
-        skel_out[j] = skel
-        total = total + dot_split(skel, transfer[j])
-    for k in range(factors.shape[0]):
-        terms_out[k] = dot_split(total, factors[k, 0])
+    rows_out[...] = dst[...].astype(bf16)
 
 
 def partner(levels_leaf, k):
@@ -78,13 +68,35 @@
 
 
 def field_kernel(
-    levels_leaf, rows, skel, terms, basis, leaf_factors, transfer, factors, out, right, local, got, held, send, recv
+    levels_leaf,
+    rows,
+    basis,
+    leaf_factors,
+    transfer,
+    factors,
+    out,
+    skel,
+    terms,
+    right,
+    basis_t,
+    local,
+    got,
+    held,
+    send,
+    recv,
 ):
     levels, rhs, rank = terms.shape
     leaves, _, leaf_len = basis.shape
     barrier = pltpu.get_barrier_semaphore()
     for k in range(levels):
         pl.semaphore_signal(barrier, inc=1, device_id=partner(levels_leaf, k), device_id_type=MESH)
+    total = jnp.zeros((rhs, rank), f32)
+    for j in range(leaves):
+        mine = dot(basis[j], rows[pl.ds(j * leaf_len, leaf_len), :]).T[:rhs]
+        skel[j] = mine
+        total = total + dot_split(mine, transfer[j])
+    for k in range(levels):
+        terms[k] = dot_split(total, factors[k, 0])
     pl.semaphore_wait(barrier, levels)
 
     copies = {}
@@ -114,8 +126,8 @@
             start(k + 1, level)
 
     def right_rows(j):
-        lane = lax.broadcasted_iota(jnp.int32, (WIDTH, WIDTH), 1)
-        lane_in = lax.broadcasted_iota(jnp.int32, (WIDTH, WIDTH), 0)
+        lane = lax.broadcasted_iota(jnp.int32, (WIDTH, WIDTH), 0)
+        lane_in = lax.broadcasted_iota(jnp.int32, (WIDTH, WIDTH), 1)
         dim = 8
         tail = rhs + 6 * dim
         source = lane
@@ -126,13 +138,15 @@
         source = jnp.where((lane >= tail + 3) & (lane < tail + 6), lane - 3, source)
         source = jnp.where((lane < rhs) | (lane >= tail + 6), -1, source)
         chosen = jnp.where(lane_in == source, 1.0, 0.0).astype(bf16)
-        span = pl.ds(j * leaf_len, leaf_len)
-        right[span, :] = dot(rows[span, :], chosen).astype(bf16)
+        right[j] = dot(chosen, rows[pl.ds(j * leaf_len, leaf_len), :], ((1,), (1,))).astype(bf16)
+
+    def turn_basis(j):
+        basis_t[j] = basis[j].T
 
     def near(j, start_row):
         span = pl.ds(j * leaf_len, leaf_len)
         mine = pl.ds(j * leaf_len + start_row, ROWS)
-        power = dot(rows[mine, :], right[span, :], ((1,), (1,)))
+        power = dot(rows[mine, :], right[j])
         out[mine, :] = dot(jnp.exp(power).astype(bf16), rows[span, :])
 
     def local_terms(h):
@@ -147,25 +161,28 @@
             local[j] = mine if h == 0 else local[j] + mine
 
     tasks = [functools.partial(right_rows, j) for j in range(leaves)]
+    tasks += [functools.partial(turn_basis, j) for j in range(leaves)]
     tasks += [functools.partial(local_terms, h) for h in range(leaf_factors.shape[1])]
     tasks += [functools.partial(near, j, s) for j in range(leaves) for s in range(0, leaf_len, ROWS)]
-    events = [(k, level) for k in range(levels) for level in reversed(range(k, levels))]
+    events = [(k, level) for k in range(levels) for level in range(k, levels)]
+    events.sort(key=lambda event: (2 * event[0] + levels - 1 - event[1], event[0]))
+    first = 2 * leaves + leaf_factors.shape[1]
     done = 0
     for i, task in enumerate(tasks):
         task()
-        while done < len(events) * (i + 1) // len(tasks):
+        while done < len(events) * (i + 1 - first) // (len(tasks) - first):
             receive(*events[done])
             done += 1
     for copy in copies.values():
         copy.wait_send()
 
-    hi = coeffs[0].astype(bf16)
-    lo = (coeffs[0] - hi.astype(f32)).astype(bf16)
+    whole = coeffs[0].T
+    hi = whole.astype(bf16)
+    lo = (whole - hi.astype(f32)).astype(bf16)
     for j in range(leaves):
         span = pl.ds(j * leaf_len, leaf_len)
-        mine = dot(transfer[j], hi, ((1,), (1,))) + dot(transfer[j], lo, ((1,), (1,)))
-        mine = (mine + local[j].T).astype(bf16)
-        out[span, :rhs] = out[span, :rhs] + dot(basis[j], mine, ((0,), (0,)))
+        mine = (dot(transfer[j], hi) + dot(transfer[j], lo) + local[j].T).astype(bf16)
+        out[span, :rhs] = out[span, :rhs] + dot(basis_t[j], mine)
 
 
 def place_kernel(order, field, out, dst):
@@ -193,27 +210,26 @@
     rhs, points = charges.shape
     leaves, rank, leaf_len = basis.shape
     levels = factors.shape[0]
-    rows, skel, terms = pl.pallas_call(
-        up_kernel,
-        out_shape=(
-            jax.ShapeDtypeStruct((points, WIDTH), bf16),
-            jax.ShapeDtypeStruct((leaves, rhs, rank), f32),
-            jax.ShapeDtypeStruct((levels, rhs, rank), f32),
-        ),
-        in_specs=[SMEM] + [VMEM] * 5,
-        out_specs=(VMEM, VMEM, VMEM),
+    rows = pl.pallas_call(
+        gather_kernel,
+        out_shape=jax.ShapeDtypeStruct((points, WIDTH), bf16),
+        in_specs=[SMEM, VMEM, VMEM],
+        out_specs=VMEM,
         scratch_shapes=[pltpu.VMEM((points, WIDTH), f32), pltpu.VMEM((points, WIDTH), f32)],
         compiler_params=params(),
-        name="up",
-    )(order, coords, charges, basis, transfer, factors)
+        name="gather",
+    )(order, coords, charges)
     levels_leaf = lax.axis_size("leaf").bit_length() - 1
     field = pl.pallas_call(
         functools.partial(field_kernel, levels_leaf),
         out_shape=jax.ShapeDtypeStruct((points, WIDTH), f32),
-        in_specs=[VMEM] * 7,
+        in_specs=[VMEM] * 5,
         out_specs=VMEM,
         scratch_shapes=[
-            pltpu.VMEM((points, WIDTH), bf16),
+            pltpu.VMEM((leaves, rhs, rank), f32),
+            pltpu.VMEM((levels, rhs, rank), f32),
+            pltpu.VMEM((leaves, WIDTH, leaf_len), bf16),
+            pltpu.VMEM((leaves, leaf_len, rank), bf16),
             pltpu.VMEM((leaves, rhs, rank), f32),
             pltpu.VMEM((levels, levels, rhs, rank), f32),
             pltpu.VMEM((levels, levels, rhs, rank), f32),
@@ -222,7 +238,7 @@
         ],
         compiler_params=params(collective_id=0, has_side_effects=True),
         name="field",
-    )(rows, skel, terms, basis, leaf_factors, transfer, factors)
+    )(rows, basis, leaf_factors, transfer, factors)
     result = pl.pallas_call(
         place_kernel,
         out_shape=jax.ShapeDtypeStruct((rhs, points), bf16),

time: 39.8 us -> 39.1 us (0.982)
  Pallas kernels: 33.7 us -> 33.1 us
    pallas_call x1, Pallas kernels: 6.32 us -> 5.03 us  [per_device(): pl.pallas_call(gather_kernel, out_shape=jax.ShapeDtypeStruct((points, WID...]
    pallas_call x1, Pallas kernels: 21.6 us -> 22.3 us  [per_device(): pl.pallas_call(functools.partial(field_kernel, levels_leaf), out_shape=ja...]
    unnamed x18 -> x16, local copies, waits for them, and re-layouts: 5.78 us -> 5.67 us
where the time goes in v3:
time: 39.1 us; the launch traced here: 38.8 us
  Pallas kernels  33.1 us (85%)
  local copies, waits for them, and re-layouts  5.67 us (15%)
    pallas_call x1, Pallas kernels, per_device(): pl.pallas_call(functools.partial(field_kernel, levels_leaf), out_shape=ja...  22.3 us
    pallas_call x1, Pallas kernels, per_device(): pl.pallas_call(place_kernel, out_shape=jax.ShapeDtypeStruct((rhs, points)...  5.76 us
    unnamed x16, local copies, waits for them, and re-layouts  5.67 us
    pallas_call x1, Pallas kernels, per_device(): pl.pallas_call(gather_kernel, out_shape=jax.ShapeDtypeStruct((points, WID...  5.03 us

profile of v3, /device:TPU:0, one launch (start us, length us, event | category | flops | bytes accessed | tf_op | source)
XLA Modules:
  0.0 38.8 jit_solution(7877447277947317389)
XLA Ops:
  0.0 0.0 copy-start
  0.0 0.0 copy-start.2
  0.0 1.1 %copy-done.2 = bf16[1,1,64,4096]{3,2,1,0:T(8,128)(2,1)S(1)} copy-done((bf16[1,1,64,4096]{3,2,1,0:T(8,128)(2,1)S(1)}, bf16[1,1,64,4096]{3,2,1,0:T(8,128)(2,1)}, u32[]{:S(2)}) %copy-start.2) | copy-done | bytes 524312
  1.1 0.0 copy-start.5
  1.1 0.9 %copy-done.5 = f32[1,1,8,4096]{3,2,1,0:T(8,128)S(1)} copy-done((f32[1,1,8,4096]{3,2,1,0:T(8,128)S(1)}, f32[1,1,8,4096]{3,2,1,0:T(8,128)}, u32[]{:S(2)}) %copy-start.5) | copy-done | bytes 131096
  2.0 0.0 copy-start.6
  2.0 0.7 %copy-done.6 = s32[1,1,4096]{2,1,0:T(1,128)S(1)} copy-done((s32[1,1,4096]{2,1,0:T(1,128)S(1)}, s32[1,1,4096]{2,1,0:T(1,128)}, u32[]{:S(2)}) %copy-start.6) | copy-done | bytes 16408
  2.8 5.0 %gather.1.rows = bf16[4096,128]{1,0:T(8,128)(2,1)S(1)} custom-call(s32[4096]{0:T(1024)S(1)} %bitcast.14, f32[8,4096]{1,0:T(8,128)S(1)} %bitcast.13, bf16[64,4096]{1,0:T(8,128)(2,1)S(1)} %bitcast.10), custom_call_target="tpu_custom_call" | custom-call | tf_op jit(solution)/shard_map/gather/pallas_call | solution.py:213
  7.8 0.0 copy-done
  7.8 0.0 copy-start.1
  7.8 1.0 %copy-done.1 = bf16[1,1,4,2,2,128,128]{6,5,4,3,2,1,0:T(8,128)(2,1)S(1)} copy-done((bf16[1,1,4,2,2,128,128]{6,5,4,3,2,1,0:T(8,128)(2,1)S(1)}, bf16[1,1,4,2,2,128,128]{6,5,4,3,2,1,0:T(8,128)(2,1)}, u32[]{:S(2)}) %copy-start.1) | copy-done | bytes 524312
  8.8 0.0 copy-start.3
  8.9 1.0 %copy-done.3 = bf16[1,1,5,2,128,128]{5,4,3,2,1,0:T(8,128)(2,1)S(1)} copy-done((bf16[1,1,5,2,128,128]{5,4,3,2,1,0:T(8,128)(2,1)S(1)}, bf16[1,1,5,2,128,128]{5,4,3,2,1,0:T(8,128)(2,1)}, u32[]{:S(2)}) %copy-start.3) | copy-done | bytes 327704
  9.8 0.0 copy-start.4
  9.8 0.9 %copy-done.4 = bf16[1,1,4,128,128]{4,3,2,1,0:T(8,128)(2,1)S(1)} copy-done((bf16[1,1,4,128,128]{4,3,2,1,0:T(8,128)(2,1)S(1)}, bf16[1,1,4,128,128]{4,3,2,1,0:T(8,128)(2,1)}, u32[]{:S(2)}) %copy-start.4) | copy-done | bytes 131096
  10.7 0.0 copy-start.7
  10.7 22.3 %field.1 = f32[4096,128]{1,0:T(8,128)S(1)} custom-call(bf16[4096,128]{1,0:T(8,128)(2,1)S(1)} %gather.1.rows, bf16[4,128,1024]{2,1,0:T(8,128)(2,1)S(1)} %bitcast.8, bf16[4,2,2,128,128]{4,3,2,1,0:T(8,128)(2,1)S(1)} %bitcast.9, bf16[4,128,128]{2,1,0:T(8,128)(2,1)S(1)} %bitcast.12, bf16[5,2,128,128]{3,2,1,0:T(8,128)(2,1)S(1)} %bitcast.11), custom_call_target="tpu_custom_call" | custom-call | tf_op jit(solution)/shard_map/field/pallas_call | solution.py:223
  33.1 0.0 copy-done.7
  33.1 5.8 %place.1 = bf16[64,4096]{1,0:T(8,128)(2,1)} custom-call(s32[4096]{0:T(1024)S(1)} %bitcast.15, f32[4096,128]{1,0:T(8,128)S(1)} %field.1), custom_call_target="tpu_custom_call" | custom-call | tf_op jit(solution)/shard_map/place/pallas_call | solution.py:242
Async XLA Ops:
  0.0 7.8 %copy-start = (bf16[1,1,4,128,1024]{4,3,2,1,0:T(8,128)(2,1)S(1)}, bf16[1,1,4,128,1024]{4,3,2,1,0:T(8,128)(2,1)}, u32[]{:S(2)}) copy-start(bf16[1,1,4,128,1024]{4,3,2,1,0:T(8,128)(2,1)} %param.10) | copy-start | bytes 3145732
  0.0 1.1 %copy-start.2 = (bf16[1,1,64,4096]{3,2,1,0:T(8,128)(2,1)S(1)}, bf16[1,1,64,4096]{3,2,1,0:T(8,128)(2,1)}, u32[]{:S(2)}) copy-start(bf16[1,1,64,4096]{3,2,1,0:T(8,128)(2,1)} %param.9) | copy-start | bytes 1572868
  1.1 0.9 %copy-start.5 = (f32[1,1,8,4096]{3,2,1,0:T(8,128)S(1)}, f32[1,1,8,4096]{3,2,1,0:T(8,128)}, u32[]{:S(2)}) copy-start(f32[1,1,8,4096]{3,2,1,0:T(8,128)} %param.7) | copy-start | bytes 393220
  2.0 0.7 %copy-start.6 = (s32[1,1,4096]{2,1,0:T(1,128)S(1)}, s32[1,1,4096]{2,1,0:T(1,128)}, u32[]{:S(2)}) copy-start(s32[1,1,4096]{2,1,0:T(1,128)} %param.8) | copy-start | bytes 49156
  7.8 1.0 %copy-start.1 = (bf16[1,1,4,2,2,128,128]{6,5,4,3,2,1,0:T(8,128)(2,1)S(1)}, bf16[1,1,4,2,2,128,128]{6,5,4,3,2,1,0:T(8,128)(2,1)}, u32[]{:S(2)}) copy-start(bf16[1,1,4,2,2,128,128]{6,5,4,3,2,1,0:T(8,128)(2,1)} %param.11) | copy-start | bytes 1572868
  8.8 1.0 %copy-start.3 = (bf16[1,1,5,2,128,128]{5,4,3,2,1,0:T(8,128)(2,1)S(1)}, bf16[1,1,5,2,128,128]{5,4,3,2,1,0:T(8,128)(2,1)}, u32[]{:S(2)}) copy-start(bf16[1,1,5,2,128,128]{5,4,3,2,1,0:T(8,128)(2,1)} %param.13) | copy-start | bytes 983044
  9.8 0.9 %copy-start.4 = (bf16[1,1,4,128,128]{4,3,2,1,0:T(8,128)(2,1)S(1)}, bf16[1,1,4,128,128]{4,3,2,1,0:T(8,128)(2,1)}, u32[]{:S(2)}) copy-start(bf16[1,1,4,128,128]{4,3,2,1,0:T(8,128)(2,1)} %param.12) | copy-start | bytes 393220
  10.7 22.3 %copy-start.7 = (s32[1,1,4096]{2,1,0:T(1,128)S(1)}, s32[1,1,4096]{2,1,0:T(1,128)}, u32[]{:S(2)}) copy-start(s32[1,1,4096]{2,1,0:T(1,128)} %param.8) | copy-start | bytes 49156

commit v4 on v3

--- a/solution.py
+++ b/solution.py
@@ -10,10 +10,10 @@
 kernel_rate = 4.0
 WIDTH = 128
 UNROLL = 32
-ROWS = 256
+ROWS = 512
 MESH = pl.DeviceIdType.MESH
 VMEM = pl.BlockSpec(memory_space=pltpu.VMEM)
-SMEM = pl.BlockSpec(memory_space=pltpu.SMEM)
+HBM = pl.BlockSpec(memory_space=pltpu.HBM)
 f32, bf16 = jnp.float32, jnp.bfloat16
 
 
@@ -34,7 +34,13 @@
     return dot(hi, w) + dot(lo, w)
 
 
-def gather_kernel(order, coords, charges, rows_out, src, dst):
+def partner(levels_leaf, k):
+    axis, bit = ("leaf", k) if k < levels_leaf else ("top", k - levels_leaf)
+    me, stride = lax.axis_index(axis), 2**bit
+    return {axis: me + stride - 2 * stride * lax.rem(lax.div(me, stride), 2)}
+
+
+def gather_rows(order, coords, charges, rows, src, dst):
     rhs, points = charges.shape
     dim = coords.shape[0]
     step = 512
@@ -58,38 +64,26 @@
         for u in range(UNROLL):
             dst[pl.ds(base + u, 1), :] = got[u]
 
-    rows_out[...] = dst[...].astype(bf16)
-
-
-def partner(levels_leaf, k):
-    axis, bit = ("leaf", k) if k < levels_leaf else ("top", k - levels_leaf)
-    me, stride = lax.axis_index(axis), 2**bit
-    return {axis: me + stride - 2 * stride * lax.rem(lax.div(me, stride), 2)}
-
-
-def field_kernel(
-    levels_leaf,
-    rows,
-    basis,
-    leaf_factors,
-    transfer,
-    factors,
-    out,
-    skel,
-    terms,
-    right,
-    basis_t,
-    local,
-    got,
-    held,
-    send,
-    recv,
-):
+    rows[...] = dst[...].astype(bf16)
+
+
+def field_kernel(levels_leaf, *refs):
+    given, field, held_in, in_sems = refs[:7], refs[7], refs[8:15], refs[15]
+    order, coords, charges, basis, leaf_factors, transfer, factors = held_in
+    src, dst, rows, skel, terms, right, basis_t, local, power, out, stage, got, held, send, recv, out_sems = refs[16:]
     levels, rhs, rank = terms.shape
     leaves, _, leaf_len = basis.shape
+    inputs = [pltpu.make_async_copy(a, b, in_sems.at[i]) for i, (a, b) in enumerate(zip(given, held_in))]
+    for i in (1, 2, 0, 3, 5, 6, 4):
+        inputs[i].start()
     barrier = pltpu.get_barrier_semaphore()
     for k in range(levels):
         pl.semaphore_signal(barrier, inc=1, device_id=partner(levels_leaf, k), device_id_type=MESH)
+    for i in (1, 2, 0):
+        inputs[i].wait()
+    gather_rows(order, coords, charges, rows, src, dst)
+    for i in (3, 5, 6):
+        inputs[i].wait()
     total = jnp.zeros((rhs, rank), f32)
     for j in range(leaves):
         mine = dot(basis[j], rows[pl.ds(j * leaf_len, leaf_len), :]).T[:rhs]
@@ -143,11 +137,18 @@
     def turn_basis(j):
         basis_t[j] = basis[j].T
 
-    def near(j, start_row):
-        span = pl.ds(j * leaf_len, leaf_len)
-        mine = pl.ds(j * leaf_len + start_row, ROWS)
-        power = dot(rows[mine, :], right[j])
-        out[mine, :] = dot(jnp.exp(power).astype(bf16), rows[span, :])
+    blocks = [(j, start_row) for j in range(leaves) for start_row in range(0, leaf_len, ROWS)]
+
+    def exponent(i):
+        j, start_row = blocks[i]
+        power[i % 2] = dot(rows[pl.ds(j * leaf_len + start_row, ROWS), :], right[j])
+
+    def near(i):
+        j, start_row = blocks[i]
+        if i + 1 < len(blocks):
+            exponent(i + 1)
+        values = jnp.exp(power[i % 2]).astype(bf16)
+        out[pl.ds(j * leaf_len + start_row, ROWS), :] = dot(values, rows[pl.ds(j * leaf_len, leaf_len), :])
 
     def local_terms(h):
         width = 2**h
@@ -162,11 +163,13 @@
 
     tasks = [functools.partial(right_rows, j) for j in range(leaves)]
     tasks += [functools.partial(turn_basis, j) for j in range(leaves)]
+    tasks += [inputs[4].wait]
     tasks += [functools.partial(local_terms, h) for h in range(leaf_factors.shape[1])]
-    tasks += [functools.partial(near, j, s) for j in range(leaves) for s in range(0, leaf_len, ROWS)]
+    tasks += [functools.partial(exponent, 0)]
+    first = len(tasks)
+    tasks += [functools.partial(near, i) for i in range(len(blocks))]
     events = [(k, level) for k in range(levels) for level in range(k, levels)]
     events.sort(key=lambda event: (2 * event[0] + levels - 1 - event[1], event[0]))
-    first = 2 * leaves + leaf_factors.shape[1]
     done = 0
     for i, task in enumerate(tasks):
         task()
@@ -176,24 +179,44 @@
     for copy in copies.values():
         copy.wait_send()
 
-    whole = coeffs[0].T
+    none = jnp.zeros((WIDTH - rhs, rank), f32)
+    whole = jnp.concatenate([coeffs[0], none], axis=0).T
     hi = whole.astype(bf16)
     lo = (whole - hi.astype(f32)).astype(bf16)
+    leaving = []
     for j in range(leaves):
         span = pl.ds(j * leaf_len, leaf_len)
-        mine = (dot(transfer[j], hi) + dot(transfer[j], lo) + local[j].T).astype(bf16)
-        out[span, :rhs] = out[span, :rhs] + dot(basis_t[j], mine)
-
-
-def place_kernel(order, field, out, dst):
+        own = jnp.concatenate([local[j], none], axis=0).T
+        mine = (dot(transfer[j], hi) + dot(transfer[j], lo) + own).astype(bf16)
+        stage[span, :] = (out[span, :] + dot(basis_t[j], mine)).astype(bf16)
+        leaving.append(pltpu.make_async_copy(stage.at[span, :], field.at[span, :], out_sems.at[j]))
+        leaving[j].start()
+    for copy in leaving:
+        copy.wait()
+
+
+def place_kernel(order_in, field_in, out, order, field, src, dst, sems):
     rhs, points = out.shape
-
-    @pl.loop(0, points // UNROLL)
-    def _(block):
-        base = pl.multiple_of(block * UNROLL, UNROLL)
-        got = [field[pl.ds(base + u, 1), :] for u in range(UNROLL)]
-        for u in range(UNROLL):
-            dst[pl.ds(order[base + u], 1), :] = got[u]
+    pieces = 4
+    size = points // pieces
+    copies = [pltpu.make_async_copy(order_in, order, sems.at[pieces])]
+    for i in range(pieces):
+        span = pl.ds(i * size, size)
+        copies.append(pltpu.make_async_copy(field_in.at[span, :], field.at[span, :], sems.at[i]))
+    for copy in copies:
+        copy.start()
+    copies[0].wait()
+    for i in range(pieces):
+        copies[i + 1].wait()
+        span = pl.ds(i * size, size)
+        src[span, :] = field[span, :].astype(f32)
+
+        @pl.loop(0, size // UNROLL)
+        def _(block):
+            base = pl.multiple_of(i * size + block * UNROLL, UNROLL)
+            got = [src[pl.ds(base + u, 1), :] for u in range(UNROLL)]
+            for u in range(UNROLL):
+                dst[pl.ds(order[base + u], 1), :] = got[u]
 
     step = 512
     for start in range(0, points, step):
@@ -201,7 +224,7 @@
 
 
 def params(**more):
-    return pltpu.CompilerParams(vmem_limit_bytes=28 * 2**20, **more)
+    return pltpu.CompilerParams(vmem_limit_bytes=60 * 2**20, **more)
 
 
 def per_device(coords, order, charges, leaf_basis, leaf_factors, transfer, block_factors):
@@ -210,41 +233,50 @@
     rhs, points = charges.shape
     leaves, rank, leaf_len = basis.shape
     levels = factors.shape[0]
-    rows = pl.pallas_call(
-        gather_kernel,
-        out_shape=jax.ShapeDtypeStruct((points, WIDTH), bf16),
-        in_specs=[SMEM, VMEM, VMEM],
-        out_specs=VMEM,
-        scratch_shapes=[pltpu.VMEM((points, WIDTH), f32), pltpu.VMEM((points, WIDTH), f32)],
-        compiler_params=params(),
-        name="gather",
-    )(order, coords, charges)
     levels_leaf = lax.axis_size("leaf").bit_length() - 1
+    inputs = (order, coords, charges, basis, leaf_factors, transfer, factors)
+    in_vmem = [pltpu.VMEM(a.shape, a.dtype) for a in inputs[1:]]
     field = pl.pallas_call(
         functools.partial(field_kernel, levels_leaf),
-        out_shape=jax.ShapeDtypeStruct((points, WIDTH), f32),
-        in_specs=[VMEM] * 5,
-        out_specs=VMEM,
+        out_shape=jax.ShapeDtypeStruct((points, WIDTH), bf16),
+        in_specs=[HBM] * len(inputs),
+        out_specs=HBM,
         scratch_shapes=[
+            pltpu.SMEM(order.shape, order.dtype),
+            *in_vmem,
+            pltpu.SemaphoreType.DMA((len(inputs),)),
+            pltpu.VMEM((points, WIDTH), f32),
+            pltpu.VMEM((points, WIDTH), f32),
+            pltpu.VMEM((points, WIDTH), bf16),
             pltpu.VMEM((leaves, rhs, rank), f32),
             pltpu.VMEM((levels, rhs, rank), f32),
             pltpu.VMEM((leaves, WIDTH, leaf_len), bf16),
             pltpu.VMEM((leaves, leaf_len, rank), bf16),
             pltpu.VMEM((leaves, rhs, rank), f32),
+            pltpu.VMEM((2, ROWS, leaf_len), f32),
+            pltpu.VMEM((points, WIDTH), f32),
+            pltpu.VMEM((points, WIDTH), bf16),
             pltpu.VMEM((levels, levels, rhs, rank), f32),
             pltpu.VMEM((levels, levels, rhs, rank), f32),
             pltpu.SemaphoreType.DMA((levels, levels)),
             pltpu.SemaphoreType.DMA((levels, levels)),
+            pltpu.SemaphoreType.DMA((leaves,)),
         ],
         compiler_params=params(collective_id=0, has_side_effects=True),
         name="field",
-    )(rows, basis, leaf_factors, transfer, factors)
+    )(*inputs)
     result = pl.pallas_call(
         place_kernel,
         out_shape=jax.ShapeDtypeStruct((rhs, points), bf16),
-        in_specs=[SMEM, VMEM],
+        in_specs=[HBM, HBM],
         out_specs=VMEM,
-        scratch_shapes=[pltpu.VMEM((points, WIDTH), f32)],
+        scratch_shapes=[
+            pltpu.SMEM(order.shape, order.dtype),
+            pltpu.VMEM((points, WIDTH), bf16),
+            pltpu.VMEM((points, WIDTH), f32),
+            pltpu.VMEM((points, WIDTH), f32),
+            pltpu.SemaphoreType.DMA((5,)),
+        ],
         compiler_params=params(),
         name="place",
     )(order, field)

time: 39.1 us -> 34.2 us (0.87)
  local copies, waits for them, and re-layouts: 5.67 us -> 0 us
  Pallas kernels: 33.1 us -> 34 us
    unnamed x16 -> x0, local copies, waits for them, and re-layouts: 5.67 us -> none
    pallas_call x1, Pallas kernels: 22.3 us -> 28 us  [per_device(): pl.pallas_call(functools.partial(field_kernel, levels_leaf), out_shape=ja...]
    pallas_call x1 -> x0, Pallas kernels: 5.03 us -> none  [per_device(): pl.pallas_call(gather_kernel, out_shape=jax.ShapeDtypeStruct((points, WID...]
where the time goes in v4:
time: 34.2 us; the launch traced here: 34 us
  Pallas kernels  34 us (99%)
    pallas_call x1, Pallas kernels, per_device(): pl.pallas_call(functools.partial(field_kernel, levels_leaf), out_shape=ja...  28 us
    pallas_call x1, Pallas kernels, per_device(): pl.pallas_call(place_kernel, out_shape=jax.ShapeDtypeStruct((rhs, points)...  5.97 us

profile of v4, /device:TPU:0, one launch (start us, length us, event | category | flops | bytes accessed | tf_op | source)
XLA Modules:
  0.0 34.0 jit_solution(11560120309191831233)
XLA Ops:
  0.0 28.0 %field.1.field_in = bf16[4096,128]{1,0:T(8,128)(2,1)} custom-call(s32[4096]{0:T(1024)} %bitcast.14, f32[8,4096]{1,0:T(8,128)} %bitcast.12, bf16[64,4096]{1,0:T(8,128)(2,1)} %bitcast.9, bf16[4,128,1024]{2,1,0:T(8,128)(2,1)} %bitcast.8, bf16[4,2,2,128,128]{4,3,2,1,0:T(8,128)(2,1)} %bitcast.10, bf16[4,128,128]{2,1,0:T(8,128)(2,1)} %bitcast.13, ...), custom_call_target="tpu_custom_call" | custom-call | tf_op jit(solution)/shard_map/field/pallas_call | solution.py:239
  28.0 6.0 %place.1 = bf16[64,4096]{1,0:T(8,128)(2,1)} custom-call(s32[4096]{0:T(1024)} %bitcast.15, bf16[4096,128]{1,0:T(8,128)(2,1)} %field.1.field_in), custom_call_target="tpu_custom_call" | custom-call | tf_op jit(solution)/shard_map/place/pallas_call | solution.py:268

commit v5 on v4

--- a/solution.py
+++ b/solution.py
@@ -32,6 +32,14 @@
     hi = x.astype(bf16)
     lo = (x - hi.astype(f32)).astype(bf16)
     return dot(hi, w) + dot(lo, w)
+
+
+def set_bits(levels_leaf, levels):
+    leaf, top = lax.axis_index("leaf"), lax.axis_index("top")
+    total = jnp.int32(0)
+    for k in range(levels):
+        total = total + (lax.rem(lax.div(leaf, 2**k), 2) if k < levels_leaf else lax.rem(lax.div(top, 2 ** (k - levels_leaf)), 2))
+    return total
 
 
 def partner(levels_leaf, k):
@@ -137,18 +145,19 @@
     def turn_basis(j):
         basis_t[j] = basis[j].T
 
-    blocks = [(j, start_row) for j in range(leaves) for start_row in range(0, leaf_len, ROWS)]
+    per_leaf = leaf_len // ROWS
+    blocks = leaves * per_leaf
 
     def exponent(i):
-        j, start_row = blocks[i]
-        power[i % 2] = dot(rows[pl.ds(j * leaf_len + start_row, ROWS), :], right[j])
-
-    def near(i):
-        j, start_row = blocks[i]
-        if i + 1 < len(blocks):
-            exponent(i + 1)
-        values = jnp.exp(power[i % 2]).astype(bf16)
-        out[pl.ds(j * leaf_len + start_row, ROWS), :] = dot(values, rows[pl.ds(j * leaf_len, leaf_len), :])
+        mine = pl.ds(pl.multiple_of(i * ROWS, ROWS), ROWS)
+        power[lax.rem(i, 2)] = dot(rows[mine, :], right[lax.div(i, per_leaf)])
+
+    def near(i, carry):
+        exponent(jnp.minimum(i + 1, blocks - 1))
+        values = jnp.exp(power[lax.rem(i, 2)]).astype(bf16)
+        leaf = pl.ds(pl.multiple_of(lax.div(i, per_leaf) * leaf_len, leaf_len), leaf_len)
+        out[pl.ds(pl.multiple_of(i * ROWS, ROWS), ROWS), :] = dot(values, rows[leaf, :])
+        return carry
 
     def local_terms(h):
         width = 2**h
@@ -161,21 +170,24 @@
             mine = dot_split(summed * 0.5 ** (h / 2.0), leaf_factors[j, h, 1])
             local[j] = mine if h == 0 else local[j] + mine
 
-    tasks = [functools.partial(right_rows, j) for j in range(leaves)]
-    tasks += [functools.partial(turn_basis, j) for j in range(leaves)]
-    tasks += [inputs[4].wait]
-    tasks += [functools.partial(local_terms, h) for h in range(leaf_factors.shape[1])]
-    tasks += [functools.partial(exponent, 0)]
-    first = len(tasks)
-    tasks += [functools.partial(near, i) for i in range(len(blocks))]
+    def prepare():
+        for j in range(leaves):
+            right_rows(j)
+            turn_basis(j)
+        for h in range(leaf_factors.shape[1]):
+            local_terms(h)
+        exponent(jnp.int32(0))
+
+    inputs[4].wait()
+    ahead = lax.div(blocks * (levels - set_bits(levels_leaf, levels)), levels)
+    pl.when(ahead > 0)(prepare)
+    lax.fori_loop(0, ahead, near, 0)
     events = [(k, level) for k in range(levels) for level in range(k, levels)]
     events.sort(key=lambda event: (2 * event[0] + levels - 1 - event[1], event[0]))
-    done = 0
-    for i, task in enumerate(tasks):
-        task()
-        while done < len(events) * (i + 1 - first) // (len(tasks) - first):
-            receive(*events[done])
-            done += 1
+    for event in events:
+        receive(*event)
+    pl.when(ahead == 0)(prepare)
+    lax.fori_loop(ahead, blocks, near, 0)
     for copy in copies.values():
         copy.wait_send()
 

time: 34.2 us -> 47.1 us (1.38)
  the two profiles are of different devices: /device:TPU:0 before, /device:TPU:31 now
where the time goes in v5:
time: 47.1 us; the launch traced here: 46.9 us
  Pallas kernels  46.9 us (100%)
    pallas_call x1, Pallas kernels, per_device(): pl.pallas_call(functools.partial(field_kernel, levels_leaf), out_shape=ja...  40.9 us
    pallas_call x1, Pallas kernels, per_device(): pl.pallas_call(place_kernel, out_shape=jax.ShapeDtypeStruct((rhs, points)...  5.98 us

profile of v5, /device:TPU:31, one launch (start us, length us, event | category | flops | bytes accessed | tf_op | source)
XLA Modules:
  0.0 46.9 jit_solution(7464414025855954502)
XLA Ops:
  0.0 40.9 %field.1.field_in = bf16[4096,128]{1,0:T(8,128)(2,1)} custom-call(s32[4096]{0:T(1024)} %bitcast.14, f32[8,4096]{1,0:T(8,128)} %bitcast.12, bf16[64,4096]{1,0:T(8,128)(2,1)} %bitcast.9, bf16[4,128,1024]{2,1,0:T(8,128)(2,1)} %bitcast.8, bf16[4,2,2,128,128]{4,3,2,1,0:T(8,128)(2,1)} %bitcast.10, bf16[4,128,128]{2,1,0:T(8,128)(2,1)} %bitcast.13, ...), custom_call_target="tpu_custom_call" | custom-call | tf_op jit(solution)/shard_map/field/pallas_call | solution.py:251
  40.9 6.0 %place.1 = bf16[64,4096]{1,0:T(8,128)(2,1)} custom-call(s32[4096]{0:T(1024)} %bitcast.15, bf16[4096,128]{1,0:T(8,128)(2,1)} %field.1.field_in), custom_call_target="tpu_custom_call" | custom-call | tf_op jit(solution)/shard_map/place/pallas_call | solution.py:280

commit v6 on v5

--- a/solution.py
+++ b/solution.py
@@ -145,19 +145,13 @@
     def turn_basis(j):
         basis_t[j] = basis[j].T
 
-    per_leaf = leaf_len // ROWS
-    blocks = leaves * per_leaf
-
-    def exponent(i):
-        mine = pl.ds(pl.multiple_of(i * ROWS, ROWS), ROWS)
-        power[lax.rem(i, 2)] = dot(rows[mine, :], right[lax.div(i, per_leaf)])
-
-    def near(i, carry):
-        exponent(jnp.minimum(i + 1, blocks - 1))
-        values = jnp.exp(power[lax.rem(i, 2)]).astype(bf16)
-        leaf = pl.ds(pl.multiple_of(lax.div(i, per_leaf) * leaf_len, leaf_len), leaf_len)
-        out[pl.ds(pl.multiple_of(i * ROWS, ROWS), ROWS), :] = dot(values, rows[leaf, :])
-        return carry
+    def near(j):
+        leaf = pl.ds(j * leaf_len, leaf_len)
+        parts = [pl.ds(j * leaf_len + start_row, ROWS) for start_row in range(0, leaf_len, ROWS)]
+        for i, part in enumerate(parts):
+            power[i] = dot(rows[part, :], right[j])
+        for i, part in enumerate(parts):
+            out[part, :] = dot(jnp.exp(power[i]).astype(bf16), rows[leaf, :])
 
     def local_terms(h):
         width = 2**h
@@ -176,18 +170,19 @@
             turn_basis(j)
         for h in range(leaf_factors.shape[1]):
             local_terms(h)
-        exponent(jnp.int32(0))
 
     inputs[4].wait()
-    ahead = lax.div(blocks * (levels - set_bits(levels_leaf, levels)), levels)
+    ahead = lax.div(leaves * (levels - set_bits(levels_leaf, levels)), levels)
     pl.when(ahead > 0)(prepare)
-    lax.fori_loop(0, ahead, near, 0)
+    for j in range(leaves):
+        pl.when(ahead > j)(functools.partial(near, j))
     events = [(k, level) for k in range(levels) for level in range(k, levels)]
     events.sort(key=lambda event: (2 * event[0] + levels - 1 - event[1], event[0]))
     for event in events:
         receive(*event)
     pl.when(ahead == 0)(prepare)
-    lax.fori_loop(ahead, blocks, near, 0)
+    for j in range(leaves):
+        pl.when(ahead <= j)(functools.partial(near, j))
     for copy in copies.values():
         copy.wait_send()
 
@@ -265,7 +260,7 @@
             pltpu.VMEM((leaves, WIDTH, leaf_len), bf16),
             pltpu.VMEM((leaves, leaf_len, rank), bf16),
             pltpu.VMEM((leaves, rhs, rank), f32),
-            pltpu.VMEM((2, ROWS, leaf_len), f32),
+            pltpu.VMEM((leaf_len // ROWS, ROWS, leaf_len), f32),
             pltpu.VMEM((points, WIDTH), f32),
             pltpu.VMEM((points, WIDTH), bf16),
             pltpu.VMEM((levels, levels, rhs, rank), f32),

time: 47.1 us -> 35.2 us (0.75)
  the two profiles are of different devices: /device:TPU:31 before, /device:TPU:10 now
where the time goes in v6:
time: 35.2 us; the launch traced here: 35 us
  Pallas kernels  34.8 us (99%)
    pallas_call x1, Pallas kernels, per_device(): pl.pallas_call(functools.partial(field_kernel, levels_leaf), out_shape=ja...  28.8 us
    pallas_call x1, Pallas kernels, per_device(): pl.pallas_call(place_kernel, out_shape=jax.ShapeDtypeStruct((rhs, points)...  5.97 us

profile of v6, /device:TPU:10, one launch (start us, length us, event | category | flops | bytes accessed | tf_op | source)
XLA Modules:
  0.0 35.0 jit_solution(9606581785748817635)
XLA Ops:
  0.0 28.8 %field.1.field_in = bf16[4096,128]{1,0:T(8,128)(2,1)} custom-call(s32[4096]{0:T(1024)} %bitcast.14, f32[8,4096]{1,0:T(8,128)} %bitcast.12, bf16[64,4096]{1,0:T(8,128)(2,1)} %bitcast.9, bf16[4,128,1024]{2,1,0:T(8,128)(2,1)} %bitcast.8, bf16[4,2,2,128,128]{4,3,2,1,0:T(8,128)(2,1)} %bitcast.10, bf16[4,128,128]{2,1,0:T(8,128)(2,1)} %bitcast.13, ...), custom_call_target="tpu_custom_call" | custom-call | tf_op jit(solution)/shard_map/field/pallas_call | solution.py:246
  28.8 6.0 %place.1 = bf16[64,4096]{1,0:T(8,128)(2,1)} custom-call(s32[4096]{0:T(1024)} %bitcast.15, bf16[4096,128]{1,0:T(8,128)(2,1)} %field.1.field_in), custom_call_target="tpu_custom_call" | custom-call | tf_op jit(solution)/shard_map/place/pallas_call | solution.py:275

commit v7 on v4

--- a/solution.py
+++ b/solution.py
@@ -1,4 +1,5 @@
 import functools
+import math
 
 import jax
 import jax.numpy as jnp
@@ -44,7 +45,7 @@
     rhs, points = charges.shape
     dim = coords.shape[0]
     step = 512
-    scale = (2.0 * kernel_rate) ** 0.5
+    scale = (2.0 * kernel_rate / math.log(2.0)) ** 0.5
     for start in range(0, points, step):
         cols = pl.ds(start, step)
         pts = coords[:, cols] * scale
@@ -106,8 +107,7 @@
         )
         copies[k, level].start()
 
-    for level in reversed(range(levels)):
-        start(0, level)
+    start(0, levels - 1)
 
     coeffs = [jnp.zeros((rhs, rank), f32)]
 
@@ -147,7 +147,7 @@
         j, start_row = blocks[i]
         if i + 1 < len(blocks):
             exponent(i + 1)
-        values = jnp.exp(power[i % 2]).astype(bf16)
+        values = jnp.exp2(power[i % 2]).astype(bf16)
         out[pl.ds(j * leaf_len + start_row, ROWS), :] = dot(values, rows[pl.ds(j * leaf_len, leaf_len), :])
 
     def local_terms(h):
@@ -161,20 +161,23 @@
             mine = dot_split(summed * 0.5 ** (h / 2.0), leaf_factors[j, h, 1])
             local[j] = mine if h == 0 else local[j] + mine
 
-    tasks = [functools.partial(right_rows, j) for j in range(leaves)]
-    tasks += [functools.partial(turn_basis, j) for j in range(leaves)]
-    tasks += [inputs[4].wait]
-    tasks += [functools.partial(local_terms, h) for h in range(leaf_factors.shape[1])]
-    tasks += [functools.partial(exponent, 0)]
-    first = len(tasks)
+    for j in range(leaves):
+        right_rows(j)
+        turn_basis(j)
+    exponent(0)
+    inputs[4].wait()
+    tasks = [functools.partial(local_terms, h) for h in range(leaf_factors.shape[1])]
     tasks += [functools.partial(near, i) for i in range(len(blocks))]
-    events = [(k, level) for k in range(levels) for level in range(k, levels)]
-    events.sort(key=lambda event: (2 * event[0] + levels - 1 - event[1], event[0]))
     done = 0
-    for i, task in enumerate(tasks):
-        task()
-        while done < len(events) * (i + 1 - first) // (len(tasks) - first):
-            receive(*events[done])
+    for turn in range(levels):
+        receive(turn, levels - 1)
+        if turn < levels - 1:
+            start(0, levels - 2 - turn)
+        for back in range(1, turn + 1):
+            if turn - back <= levels - 1 - back:
+                receive(turn - back, levels - 1 - back)
+        while done < len(tasks) and done * (levels - 1) < len(tasks) * (turn + 1):
+            tasks[done]()
             done += 1
     for copy in copies.values():
         copy.wait_send()

time: 34.2 us -> 35.8 us (1.047)
  Pallas kernels: 34 us -> 35.6 us
    pallas_call x1, Pallas kernels: 28 us -> 29.6 us  [per_device(): pl.pallas_call(functools.partial(field_kernel, levels_leaf), out_shape=ja...]
where the time goes in v7:
time: 35.8 us; the launch traced here: 35.6 us
  Pallas kernels  35.6 us (99%)
    pallas_call x1, Pallas kernels, per_device(): pl.pallas_call(functools.partial(field_kernel, levels_leaf), out_shape=ja...  29.6 us
    pallas_call x1, Pallas kernels, per_device(): pl.pallas_call(place_kernel, out_shape=jax.ShapeDtypeStruct((rhs, points)...  5.97 us

profile of v7, /device:TPU:0, one launch (start us, length us, event | category | flops | bytes accessed | tf_op | source)
XLA Modules:
  0.0 35.6 jit_solution(6592142659164029199)
XLA Ops:
  0.0 29.6 %field.1.field_in = bf16[4096,128]{1,0:T(8,128)(2,1)} custom-call(s32[4096]{0:T(1024)} %bitcast.14, f32[8,4096]{1,0:T(8,128)} %bitcast.12, bf16[64,4096]{1,0:T(8,128)(2,1)} %bitcast.9, bf16[4,128,1024]{2,1,0:T(8,128)(2,1)} %bitcast.8, bf16[4,2,2,128,128]{4,3,2,1,0:T(8,128)(2,1)} %bitcast.10, bf16[4,128,128]{2,1,0:T(8,128)(2,1)} %bitcast.13, ...), custom_call_target="tpu_custom_call" | custom-call | tf_op jit(solution)/shard_map/field/pallas_call | solution.py:242
  29.6 6.0 %place.1 = bf16[64,4096]{1,0:T(8,128)(2,1)} custom-call(s32[4096]{0:T(1024)} %bitcast.15, bf16[4096,128]{1,0:T(8,128)(2,1)} %field.1.field_in), custom_call_target="tpu_custom_call" | custom-call | tf_op jit(solution)/shard_map/place/pallas_call | solution.py:271

commit v8 on v4

--- a/solution.py
+++ b/solution.py
@@ -1,4 +1,5 @@
 import functools
+import math
 
 import jax
 import jax.numpy as jnp
@@ -34,17 +35,31 @@
     return dot(hi, w) + dot(lo, w)
 
 
-def partner(levels_leaf, k):
-    axis, bit = ("leaf", k) if k < levels_leaf else ("top", k - levels_leaf)
-    me, stride = lax.axis_index(axis), 2**bit
-    return {axis: me + stride - 2 * stride * lax.rem(lax.div(me, stride), 2)}
+def partner(levels_leaf, bits):
+    place = {}
+    for k in bits:
+        axis, bit = ("leaf", k) if k < levels_leaf else ("top", k - levels_leaf)
+        me, stride = lax.axis_index(axis), 2**bit
+        place[axis] = place.get(axis, me) + stride - 2 * stride * lax.rem(lax.div(me, stride), 2)
+    return place
+
+
+def stages_of(levels):
+    stages = []
+    for low in range(0, levels, 2):
+        stages.append([(low,), (low + 1,), (low, low + 1)] if low + 1 < levels else [(low,)])
+    return stages
+
+
+def takes(bits, level, stage):
+    return level >= bits[-1] and not (level == 2 * stage + 1 and bits == (2 * stage,))
 
 
 def gather_rows(order, coords, charges, rows, src, dst):
     rhs, points = charges.shape
     dim = coords.shape[0]
     step = 512
-    scale = (2.0 * kernel_rate) ** 0.5
+    scale = (2.0 * kernel_rate / math.log(2.0)) ** 0.5
     for start in range(0, points, step):
         cols = pl.ds(start, step)
         pts = coords[:, cols] * scale
@@ -77,8 +92,10 @@
     for i in (1, 2, 0, 3, 5, 6, 4):
         inputs[i].start()
     barrier = pltpu.get_barrier_semaphore()
-    for k in range(levels):
-        pl.semaphore_signal(barrier, inc=1, device_id=partner(levels_leaf, k), device_id_type=MESH)
+    stages = stages_of(levels)
+    others = [bits for stage in stages for bits in stage]
+    for bits in others:
+        pl.semaphore_signal(barrier, inc=1, device_id=partner(levels_leaf, bits), device_id_type=MESH)
     for i in (1, 2, 0):
         inputs[i].wait()
     gather_rows(order, coords, charges, rows, src, dst)
@@ -91,33 +108,40 @@
         total = total + dot_split(mine, transfer[j])
     for k in range(levels):
         terms[k] = dot_split(total, factors[k, 0])
-    pl.semaphore_wait(barrier, levels)
+    pl.semaphore_wait(barrier, len(others))
 
     copies = {}
 
-    def start(k, level):
-        copies[k, level] = pltpu.make_async_remote_copy(
-            src_ref=terms.at[level] if k == 0 else held.at[k, level],
-            dst_ref=got.at[k, level],
-            send_sem=send.at[k, level],
-            recv_sem=recv.at[k, level],
-            device_id=partner(levels_leaf, k),
-            device_id_type=MESH,
-        )
-        copies[k, level].start()
+    def start(stage, level):
+        for i, bits in enumerate(stages[stage]):
+            if takes(bits, level, stage):
+                copies[stage, i, level] = pltpu.make_async_remote_copy(
+                    src_ref=terms.at[level] if stage == 0 else held.at[stage, level],
+                    dst_ref=got.at[stage, i, level],
+                    send_sem=send.at[stage, i, level],
+                    recv_sem=recv.at[stage, i, level],
+                    device_id=partner(levels_leaf, bits),
+                    device_id_type=MESH,
+                )
+                copies[stage, i, level].start()
 
     for level in reversed(range(levels)):
         start(0, level)
 
     coeffs = [jnp.zeros((rhs, rank), f32)]
 
-    def receive(k, level):
-        copies[k, level].wait_recv()
-        if level == k:
-            coeffs[0] = coeffs[0] + dot_split(got[k, k] * 0.5 ** (k / 2.0), factors[k, 1])
+    def receive(stage, level):
+        heard = None
+        for i, bits in enumerate(stages[stage]):
+            if takes(bits, level, stage):
+                copies[stage, i, level].wait_recv()
+                part = got[stage, i, level]
+                heard = part if heard is None else heard + part
+        if level <= 2 * stage + 1:
+            coeffs[0] = coeffs[0] + dot_split(heard * 0.5 ** (level / 2.0), factors[level, 1])
         else:
-            held[k + 1, level] = (terms[level] if k == 0 else held[k, level]) + got[k, level]
-            start(k + 1, level)
+            held[stage + 1, level] = (terms[level] if stage == 0 else held[stage, level]) + heard
+            start(stage + 1, level)
 
     def right_rows(j):
         lane = lax.broadcasted_iota(jnp.int32, (WIDTH, WIDTH), 0)
@@ -147,7 +171,7 @@
         j, start_row = blocks[i]
         if i + 1 < len(blocks):
             exponent(i + 1)
-        values = jnp.exp(power[i % 2]).astype(bf16)
+        values = jnp.exp2(power[i % 2]).astype(bf16)
         out[pl.ds(j * leaf_len + start_row, ROWS), :] = dot(values, rows[pl.ds(j * leaf_len, leaf_len), :])
 
     def local_terms(h):
@@ -168,12 +192,12 @@
     tasks += [functools.partial(exponent, 0)]
     first = len(tasks)
     tasks += [functools.partial(near, i) for i in range(len(blocks))]
-    events = [(k, level) for k in range(levels) for level in range(k, levels)]
+    events = [(t, level) for t in range(len(stages)) for level in range(2 * t, levels)]
     events.sort(key=lambda event: (2 * event[0] + levels - 1 - event[1], event[0]))
     done = 0
     for i, task in enumerate(tasks):
         task()
-        while done < len(events) * (i + 1 - first) // (len(tasks) - first):
+        while done < min(len(events), len(events) * (i + 1 - first) // (len(tasks) - first - 1)):
             receive(*events[done])
             done += 1
     for copy in copies.values():
@@ -234,6 +258,7 @@
     leaves, rank, leaf_len = basis.shape
     levels = factors.shape[0]
     levels_leaf = lax.axis_size("leaf").bit_length() - 1
+    stages = len(stages_of(levels))
     inputs = (order, coords, charges, basis, leaf_factors, transfer, factors)
     in_vmem = [pltpu.VMEM(a.shape, a.dtype) for a in inputs[1:]]
     field = pl.pallas_call(
@@ -256,10 +281,10 @@
             pltpu.VMEM((2, ROWS, leaf_len), f32),
             pltpu.VMEM((points, WIDTH), f32),
             pltpu.VMEM((points, WIDTH), bf16),
-            pltpu.VMEM((levels, levels, rhs, rank), f32),
-            pltpu.VMEM((levels, levels, rhs, rank), f32),
-            pltpu.SemaphoreType.DMA((levels, levels)),
-            pltpu.SemaphoreType.DMA((levels, levels)),
+            pltpu.VMEM((stages, 3, levels, rhs, rank), f32),
+            pltpu.VMEM((stages, levels, rhs, rank), f32),
+            pltpu.SemaphoreType.DMA((stages, 3, levels)),
+            pltpu.SemaphoreType.DMA((stages, 3, levels)),
             pltpu.SemaphoreType.DMA((leaves,)),
         ],
         compiler_params=params(collective_id=0, has_side_effects=True),

time: 34.2 us -> 32.2 us (0.942)
  the two profiles are of different devices: /device:TPU:0 before, /device:TPU:1 now
where the time goes in v8:
time: 32.2 us; the launch traced here: 32 us
  Pallas kernels  32 us (99%)
    pallas_call x1, Pallas kernels, per_device(): pl.pallas_call(functools.partial(field_kernel, levels_leaf), out_shape=ja...  26 us
    pallas_call x1, Pallas kernels, per_device(): pl.pallas_call(place_kernel, out_shape=jax.ShapeDtypeStruct((rhs, points)...  5.97 us

profile of v8, /device:TPU:1, one launch (start us, length us, event | category | flops | bytes accessed | tf_op | source)
XLA Modules:
  0.0 32.0 jit_solution(11291469615847048874)
XLA Ops:
  0.0 26.0 %field.1.field_in = bf16[4096,128]{1,0:T(8,128)(2,1)} custom-call(s32[4096]{0:T(1024)} %bitcast.14, f32[8,4096]{1,0:T(8,128)} %bitcast.12, bf16[64,4096]{1,0:T(8,128)(2,1)} %bitcast.9, bf16[4,128,1024]{2,1,0:T(8,128)(2,1)} %bitcast.8, bf16[4,2,2,128,128]{4,3,2,1,0:T(8,128)(2,1)} %bitcast.10, bf16[4,128,128]{2,1,0:T(8,128)(2,1)} %bitcast.13, ...), custom_call_target="tpu_custom_call" | custom-call | tf_op jit(solution)/shard_map/field/pallas_call | solution.py:264
  26.0 6.0 %place.1 = bf16[64,4096]{1,0:T(8,128)(2,1)} custom-call(s32[4096]{0:T(1024)} %bitcast.15, bf16[4096,128]{1,0:T(8,128)(2,1)} %field.1.field_in), custom_call_target="tpu_custom_call" | custom-call | tf_op jit(solution)/shard_map/place/pallas_call | solution.py:293

commit v9 on v8

--- a/solution.py
+++ b/solution.py
@@ -219,7 +219,7 @@
         copy.wait()
 
 
-def place_kernel(order_in, field_in, out, order, field, src, dst, sems):
+def place_kernel(order_in, field_in, out, order, field, src, dst, turned, sems, out_sems):
     rhs, points = out.shape
     pieces = 4
     size = points // pieces
@@ -242,9 +242,15 @@
             for u in range(UNROLL):
                 dst[pl.ds(order[base + u], 1), :] = got[u]
 
-    step = 512
-    for start in range(0, points, step):
-        out[:, pl.ds(start, step)] = dst[pl.ds(start, step), :].T[:rhs].astype(bf16)
+    step = points // 4
+    leaving = []
+    for i in range(4):
+        span = pl.ds(i * step, step)
+        turned[:, span] = dst[span, :].astype(bf16).T[:rhs]
+        leaving.append(pltpu.make_async_copy(turned.at[:, span], out.at[:, span], out_sems.at[i]))
+        leaving[i].start()
+    for copy in leaving:
+        copy.wait()
 
 
 def params(**more):
@@ -294,13 +300,15 @@
         place_kernel,
         out_shape=jax.ShapeDtypeStruct((rhs, points), bf16),
         in_specs=[HBM, HBM],
-        out_specs=VMEM,
+        out_specs=HBM,
         scratch_shapes=[
             pltpu.SMEM(order.shape, order.dtype),
             pltpu.VMEM((points, WIDTH), bf16),
             pltpu.VMEM((points, WIDTH), f32),
             pltpu.VMEM((points, WIDTH), f32),
+            pltpu.VMEM((rhs, points), bf16),
             pltpu.SemaphoreType.DMA((5,)),
+            pltpu.SemaphoreType.DMA((4,)),
         ],
         compiler_params=params(),
         name="place",

time: 32.2 us -> 32.1 us (level)
  no operation moved by 1% of the time
where the time goes in v9:
time: 32.1 us; the launch traced here: 31.9 us
  Pallas kernels  31.9 us (99%)
    pallas_call x1, Pallas kernels, per_device(): pl.pallas_call(functools.partial(field_kernel, levels_leaf), out_shape=ja...  26 us
    pallas_call x1, Pallas kernels, per_device(): pl.pallas_call(place_kernel, out_shape=jax.ShapeDtypeStruct((rhs, points)...  5.86 us

profile of v9, /device:TPU:1, one launch (start us, length us, event | category | flops | bytes accessed | tf_op | source)
XLA Modules:
  0.0 31.9 jit_solution(15170785516163486253)
XLA Ops:
  0.0 26.0 %field.1.field_in = bf16[4096,128]{1,0:T(8,128)(2,1)} custom-call(s32[4096]{0:T(1024)} %bitcast.14, f32[8,4096]{1,0:T(8,128)} %bitcast.12, bf16[64,4096]{1,0:T(8,128)(2,1)} %bitcast.9, bf16[4,128,1024]{2,1,0:T(8,128)(2,1)} %bitcast.8, bf16[4,2,2,128,128]{4,3,2,1,0:T(8,128)(2,1)} %bitcast.10, bf16[4,128,128]{2,1,0:T(8,128)(2,1)} %bitcast.13, ...), custom_call_target="tpu_custom_call" | custom-call | tf_op jit(solution)/shard_map/field/pallas_call | solution.py:270
  26.0 5.9 %place.1 = bf16[64,4096]{1,0:T(8,128)(2,1)} custom-call(s32[4096]{0:T(1024)} %bitcast.15, bf16[4096,128]{1,0:T(8,128)(2,1)} %field.1.field_in), custom_call_target="tpu_custom_call" | custom-call | tf_op jit(solution)/shard_map/place/pallas_call | solution.py:299
